TPU v7x, 32 devices: a whole 2x2x4 slice. The times are simulated.
32 devices in a mesh: dp: 4 (over z), ep: 8 (over y, x, core).
Axes of the slice: x: 2, y: 2, z: 4, core: 2. Of those that a mesh axis runs over, the one named last changes fastest.
Arguments:
- queries: bfloat16 [512, 2, 8192], P(('dp', 'ep')), may hold values from -150 to 150
- keys_new: bfloat16 [512, 2, 512], P(('dp', 'ep')), may hold values from -5 to 5
- values_new: bfloat16 [512, 2, 512], P(('dp', 'ep')), may hold values from -5 to 5
- importance: float32 [512, 2, 4], P(('dp', 'ep')), may hold values from 0.25 to 4
- merge_flags: int32 [512, 2, 4], P(('dp', 'ep')), may hold values 0 or 1
- key_cache: bfloat16 [512, 512, 512], P(('dp', 'ep')), may hold values from -5.1 to 5.1
- value_cache: bfloat16 [512, 512, 512], P(('dp', 'ep')), may hold values from -5 to 5
- last_weight: float32 [512, 4], P(('dp', 'ep')), may hold values from 0.5 to 8
- lengths: int32 [512], P(('dp', 'ep')), may hold values from 2 to 510, as said below
- residual: bfloat16 [512, 2, 2048], P(('dp', 'ep')), may hold values from -6 to 6
- o_weight: bfloat16 [8192, 2048], P('ep'), may hold values from -0.0625 to 0.0625
- norm_gain: float32 [2048], replicated, may hold values from 0.5 to 1.5
- expert_gate_up: bfloat16 [32, 2048, 1536], P(('dp', 'ep')), may hold values from -0.125 to 0.125
- expert_down: bfloat16 [32, 768, 2048], P(('dp', 'ep')), may hold values from -0.21875 to 0.21875
- routes: int32 [512, 2, 8], P(('dp', 'ep')), may hold values from 0 to 31, all different within a row; in each aligned block of 32 rows (0 to 31, 32 to 63, ..., all dimensions but the last counted through in order) at most 16 rows name the same one
- route_weights: float32 [512, 2, 8], P(('dp', 'ep')), may hold values from 0.05 to 0.5
Outputs:
- attended: bfloat16 [512, 2, 8192], P(('dp', 'ep'))
- layer_out: bfloat16 [512, 2, 2048], P(('dp', 'ep'))
Inputs may be any that keep to these rules, and one draw needn't show every extreme that they name: `lengths`: the largest length is 510 in every draw. `routes`: each token names 8 different experts; among the rows of one device (32 tokens) no expert is named more than 16 times, a bound that some block reaches.
All inputs are finite; a program needn't handle non-finite values. No bound on the sum of `merge_flags` on one device may be relied on, other than what follows from the above.
Results may differ from a plain program's by a relative error of at most 0.018.
Values may be sent and summed in bfloat16 or wider, within the bound.
A program may use at most 128 MiB of HBM per device.

v0:
```python
import math

import jax
import jax.numpy as jnp
from jax import lax
from jax.sharding import PartitionSpec as P

EPS = 1e-06


def build_tail(
    key_cache,
    value_cache,
    lengths,
    keys_new,
    values_new,
    importance,
    merge_flags,
    last_weight,
    heads_kv,
):
    requests, steps, features = keys_new.shape
    head_dim = features // heads_kv
    last_slot = lengths - 1

    def take_slot(cache_rows, position):
        return lax.dynamic_slice_in_dim(cache_rows, position, 1, 0)

    first_keys = jax.vmap(take_slot)(key_cache, last_slot)
    first_values = jax.vmap(take_slot)(value_cache, last_slot)
    blank = jnp.zeros((requests, steps, features), jnp.bfloat16)
    tail_keys = jnp.concatenate([first_keys, blank], axis=1).reshape(
        requests, steps + 1, heads_kv, head_dim
    )
    tail_values = jnp.concatenate([first_values, blank], axis=1).reshape(
        requests, steps + 1, heads_kv, head_dim
    )
    filled = jnp.ones((requests, heads_kv), jnp.int32)
    weight = last_weight
    positions = jnp.arange(steps + 1, dtype=jnp.int32)
    live_counts = []
    key_states = []
    value_states = []
    for step in range(steps):
        merging = merge_flags[:, step] == 1
        portion = importance[:, step]
        target = jnp.where(merging, filled - 1, filled)
        picked = positions[None, :, None] == target[:, None, :]

        def settle(tail, fresh):
            fresh = fresh.reshape(requests, heads_kv, head_dim).astype(jnp.float32)
            former = jnp.sum(jnp.where(picked[..., None], tail.astype(jnp.float32), 0.0), axis=1)
            blended = (weight[..., None] * former + portion[..., None] * fresh) / (
                weight + portion
            )[..., None]
            new_row = jnp.where(merging[..., None], blended, fresh).astype(jnp.bfloat16)
            return jnp.where(picked[..., None], new_row[:, None], tail)

        tail_keys = settle(tail_keys, keys_new[:, step])
        tail_values = settle(tail_values, values_new[:, step])
        weight = jnp.where(merging, weight + portion, portion)
        filled = jnp.where(merging, filled, filled + 1)
        live_counts.append(filled)
        key_states.append(tail_keys)
        value_states.append(tail_values)
    return (
        jnp.stack(key_states, axis=1),
        jnp.stack(value_states, axis=1),
        jnp.stack(live_counts, axis=2),
    )


def first_pass(keys, queries, slot_order, limits, block, scale):
    requests, slots = (keys.shape[0], keys.shape[1])
    heads_kv, rows = (queries.shape[1], queries.shape[2])
    usable = jnp.sum((slot_order[None, :] < limits[:, None]).astype(jnp.int32), axis=1)
    blocks = (jnp.max(usable) + block - 1) // block
    initial = jnp.full((requests, heads_kv, rows, slots), -jnp.inf, jnp.float32)

    def first_advance(index, buffer):
        start = index * block
        key_block = lax.dynamic_slice_in_dim(keys, start, block, 1)
        scores = (
            jnp.einsum("ngqd,nkgd->ngqk", queries, key_block, preferred_element_type=jnp.float32)
            * scale
        )
        order_block = lax.dynamic_slice_in_dim(slot_order, start, block, 0)
        valid = order_block[None, :] < limits[:, None]
        scores = jnp.where(valid[:, None, None, :], scores, -jnp.inf)
        return lax.dynamic_update_slice_in_dim(buffer, scores, start, 3)

    return (lax.fori_loop(0, blocks, first_advance, initial), blocks)


def second_pass(values, buffer, highest, blocks, block):
    requests, heads_kv, rows = (buffer.shape[0], buffer.shape[1], buffer.shape[2])
    head_dim = values.shape[3]

    def second_advance(index, carry):
        summed, totals = carry
        start = index * block
        scores = lax.dynamic_slice_in_dim(buffer, start, block, 3)
        raw = jnp.exp(scores - highest[..., None])
        totals = totals + jnp.sum(raw, axis=3)
        value_block = lax.dynamic_slice_in_dim(values, start, block, 1)
        summed = summed + jnp.einsum(
            "ngqk,nkgd->ngqd",
            raw.astype(jnp.bfloat16),
            value_block,
            preferred_element_type=jnp.float32,
        )
        return (summed, totals)

    initial = (
        jnp.zeros((requests, heads_kv, rows, head_dim), jnp.float32),
        jnp.zeros((requests, heads_kv, rows), jnp.float32),
    )
    return lax.fori_loop(0, blocks, second_advance, initial)


def run_experts(arriving, expert_gate_up, expert_down):
    hidden_units = expert_down.shape[1]
    both = jnp.einsum(
        "sjcd,jdf->sjcf", arriving, expert_gate_up, preferred_element_type=jnp.float32
    )
    active = (jax.nn.silu(both[..., :hidden_units]) * both[..., hidden_units:]).astype(jnp.bfloat16)
    return jnp.einsum(
        "sjcf,jfd->sjcd", active, expert_down, preferred_element_type=jnp.float32
    ).astype(jnp.bfloat16)


def shards(
    queries,
    keys_new,
    values_new,
    importance,
    merge_flags,
    key_cache,
    value_cache,
    last_weight,
    lengths,
    residual,
    o_weight,
    norm_gain,
    expert_gate_up,
    expert_down,
    routes,
    route_weights,
):
    heads_kv = last_weight.shape[1]
    requests, steps, query_width = queries.shape
    features = keys_new.shape[2]
    head_dim = features // heads_kv
    heads_query = query_width // head_dim
    group = heads_query // heads_kv
    slots_all = key_cache.shape[1]
    scale = 1.0 / math.sqrt(head_dim)
    tail_keys, tail_values, live = build_tail(
        key_cache,
        value_cache,
        lengths,
        keys_new,
        values_new,
        importance,
        merge_flags,
        last_weight,
        heads_kv,
    )
    grouped = (
        queries.reshape(requests, steps, heads_kv, group, head_dim)
        .transpose(0, 2, 1, 3, 4)
        .reshape(requests, heads_kv, steps * group, head_dim)
    )
    per_step = grouped.reshape(requests, heads_kv, steps, group, head_dim)
    tail_scores = (
        jnp.einsum("ngtqd,ntsgd->ngtqs", per_step, tail_keys, preferred_element_type=jnp.float32)
        * scale
    )
    tail_scores = tail_scores.reshape(requests, heads_kv, steps * group, steps + 1)
    live_rows = jnp.repeat(live, group, axis=2)
    tail_valid = jnp.arange(steps + 1, dtype=jnp.int32)[None, None, None, :] < live_rows[..., None]
    tail_scores = jnp.where(tail_valid, tail_scores, -jnp.inf)
    tail_highest = jnp.max(tail_scores, axis=3)
    limits = lengths - 1
    keys_grid = key_cache.reshape(requests, slots_all, heads_kv, head_dim)
    values_grid = value_cache.reshape(requests, slots_all, heads_kv, head_dim)
    block = math.gcd(slots_all, 256)
    slot_order = jnp.arange(slots_all, dtype=jnp.int32)
    buffer, blocks = first_pass(keys_grid, grouped, slot_order, limits, block, scale)
    highest = jnp.maximum(jnp.max(buffer, axis=3), tail_highest)
    summed, totals = second_pass(values_grid, buffer, highest, blocks, block)
    tail_raw = jnp.exp(tail_scores - highest[..., None])
    totals = totals + jnp.sum(tail_raw, axis=3)
    tail_weights = tail_raw.astype(jnp.bfloat16).reshape(
        requests, heads_kv, steps, group, steps + 1
    )
    tail_sums = jnp.einsum(
        "ngtqs,ntsgd->ngtqd", tail_weights, tail_values, preferred_element_type=jnp.float32
    )
    summed = summed + tail_sums.reshape(requests, heads_kv, steps * group, head_dim)
    attended = (summed / totals[..., None]).astype(jnp.bfloat16)
    attended = (
        attended.reshape(requests, heads_kv, steps, group, head_dim)
        .transpose(0, 2, 1, 3, 4)
        .reshape(requests, steps, query_width)
    )
    members = lax.axis_size("ep")
    rows = requests * steps
    spread = lax.all_to_all(
        attended.reshape(rows, members, query_width // members),
        "ep",
        split_axis=1,
        concat_axis=0,
        tiled=True,
    )
    spread = spread.reshape(members * rows, query_width // members)
    projected = lax.psum_scatter(
        jnp.dot(spread, o_weight, preferred_element_type=jnp.float32),
        "ep",
        scatter_dimension=0,
        tiled=True,
    )
    width = o_weight.shape[1]
    mixed = residual.reshape(rows, width).astype(jnp.float32) + projected
    normed = (
        mixed * lax.rsqrt(jnp.mean(mixed * mixed, axis=1, keepdims=True) + EPS) * norm_gain
    ).astype(jnp.bfloat16)
    experts_local = expert_gate_up.shape[0]
    dp_size = lax.axis_size("dp")
    experts_all = experts_local * dp_size * members
    top_k = routes.shape[2]
    capacity = max(2, 2 * rows * top_k // experts_all)
    chosen = routes.reshape(rows * top_k)
    sequence = jnp.arange(rows * top_k, dtype=jnp.int32)
    earlier = sequence[:, None] > sequence[None, :]
    rank = jnp.sum(((chosen[:, None] == chosen[None, :]) & earlier).astype(jnp.int32), axis=1)
    target = chosen * capacity + rank
    placing = (
        jnp.arange(experts_all * capacity, dtype=jnp.int32)[:, None] == target[None, :]
    ).reshape(experts_all * capacity, rows, top_k)
    placing = jnp.any(placing, axis=2).astype(jnp.bfloat16)
    outgoing = jnp.dot(placing, normed, preferred_element_type=jnp.float32).astype(jnp.bfloat16)
    arrived = lax.all_to_all(
        outgoing.reshape(experts_all, capacity, width),
        ("dp", "ep"),
        split_axis=0,
        concat_axis=0,
        tiled=True,
    )
    depth = arrived.shape[1]
    sources = arrived.shape[0] // experts_local
    answer = run_experts(
        arrived.reshape(sources, experts_local, depth, width), expert_gate_up, expert_down
    )
    returned = lax.all_to_all(
        answer.reshape(sources * experts_local, depth, width),
        ("dp", "ep"),
        split_axis=0,
        concat_axis=0,
        tiled=True,
    )
    results = returned.reshape(experts_all * capacity, width)[target].reshape(rows, top_k, width)
    blended = jnp.sum(route_weights.reshape(rows, top_k, 1) * results.astype(jnp.float32), axis=1)
    layer_out = (mixed + blended).astype(jnp.bfloat16).reshape(requests, steps, width)
    return (attended, layer_out)


def solution(mesh):
    return jax.shard_map(
        shards,
        mesh=mesh,
        in_specs=(
            P(("dp", "ep"), None, None),
            P(("dp", "ep"), None, None),
            P(("dp", "ep"), None, None),
            P(("dp", "ep"), None, None),
            P(("dp", "ep"), None, None),
            P(("dp", "ep"), None, None),
            P(("dp", "ep"), None, None),
            P(("dp", "ep"), None),
            P(("dp", "ep")),
            P(("dp", "ep"), None, None),
            P("ep", None),
            P(),
            P(("dp", "ep"), None, None),
            P(("dp", "ep"), None, None),
            P(("dp", "ep"), None, None),
            P(("dp", "ep"), None, None),
        ),
        out_specs=(P(("dp", "ep"), None, None), P(("dp", "ep"), None, None)),
        check_vma=False,
    )
```

profile of v0, /device:TPU:0, one launch (start us, length us, event | category | flops | bytes accessed | tf_op | source)
XLA Modules:
  0.0 302.2 jit_solution(3669324320763978403)
XLA Ops:
  7.2 1.4 select_bitcast_fusion
  8.6 1.2 add_select_fusion
  9.9 1.3 slice_bitcast_fusion
  11.2 1.3 fusion.65
  16.0 12.3 %copy.117 = bf16[16,512,512]{1,2,0:T(8,128)(2,1)} copy(bf16[16,512,512]{2,1,0:T(8,128)(2,1)} %param.25) | data formatting | bytes 16777216 | tf_op args[5]
  28.4 1.5 gather_fusion.1
  29.8 1.5 gather_fusion.2
  31.3 12.3 %copy.135 = bf16[16,512,512]{1,2,0:T(8,128)(2,1)} copy(bf16[16,512,512]{2,1,0:T(8,128)(2,1)} %param.26) | data formatting | bytes 16777216 | tf_op args[6]
  50.5 0.8 select_reduce_fusion
  51.9 1.3 copy.131
  53.3 1.3 copy.134
  54.6 1.2 copy.130
  55.8 1.3 copy.133
  59.2 2.2 reshape.374
  61.5 1.9 copy.118
  63.4 2.5 broadcast_in_dim.174
  65.8 9.2 %while.22 = (s32[]{:T(128)}, f32[16,4,32,512]{3,2,1,0:T(8,128)}, s32[]{:T(128)}, s32[512]{0:T(512)S(1)}, s32[16]{0:T(128)S(1)}, /*index=5*/bf16[16,512,4,128]{1,...) while((s32[]{:T(128)}, f32[16,4,32,512]{3,2,1,0:T(8,128)}, ...), condition=%wide.region_3.4_spmd, body=%wide.region_2.3_spmd.sunk | while | flops 135270400 | bytes 6828255 | solution.py:92
  66.0 4.5 %bitcast_dynamic-update-slice_fusion.2 = f32[16,4,32,512]{3,2,1,0:T(8,128)} fusion(f32[16,4,32,512]{3,2,1,0:T(8,128)} %get-tuple-element.305, s32[]{:T(128)S(6)} %select_n.274, bf16[16,4,32,128]{3,2,1,0:T(8,128)(2,1)} %get-tuple-element.321, bf16[16,512,4,128]{1,3,2,0:T(8,128)(2,1)} %get-tuple-element.320, ...), kind=kOutput, calls=%fused_computation.5.clone.1 | convolution fusion | flops 135266304 | bytes 6820864 | tf_op jit(solution)/shard_map/while/body/ngqd,nkgd->ngqk/dot_general | solution.py:84
  70.6 4.4 %bitcast_dynamic-update-slice_fusion.2 = f32[16,4,32,512]{3,2,1,0:T(8,128)} fusion(f32[16,4,32,512]{3,2,1,0:T(8,128)} %get-tuple-element.305, s32[]{:T(128)S(6)} %select_n.274, bf16[16,4,32,128]{3,2,1,0:T(8,128)(2,1)} %get-tuple-element.321, bf16[16,512,4,128]{1,3,2,0:T(8,128)(2,1)} %get-tuple-element.320, ...), kind=kOutput, calls=%fused_computation.5.clone.1 | convolution fusion | flops 135266304 | bytes 6820864 | tf_op jit(solution)/shard_map/while/body/ngqd,nkgd->ngqk/dot_general | solution.py:84
  75.1 2.6 reduce_max.32
  78.4 0.9 fusion.57
  79.3 0.9 fusion.58
  80.2 0.9 broadcast_select_fusion
  81.0 1.5 fusion.70
  83.9 0.9 max.10
  84.8 0.9 fusion.36
  85.7 1.5 reduce_sum.114
  88.0 1.2 broadcast_in_dim.172
  89.2 13.3 %while.23 = (s32[]{:T(128)}, f32[16,4,32,128]{3,2,1,0:T(8,128)}, f32[16,4,32]{2,1,0:T(4,128)S(1)}, s32[]{:T(128)}, f32[16,4,32,512]{3,2,1,0:T(8,128)}, /*index=5...) while((s32[]{:T(128)}, f32[16,4,32,128]{3,2,1,0:T(8,128)}, ...), condition=%wide.region_10.11_spmd, body=%wide.region_8.10_spmd.sunk | while | flops 136577024 | bytes 27313340 | solution.py:118
  89.2 5.9 %fusion.87 = f32[16,4,32,128]{3,2,1,0:T(8,128)} fusion(f32[16,4,32,128]{3,2,1,0:T(8,128)} %get-tuple-element.338, bf16[16,512,4,128]{1,3,2,0:T(8,128)(2,1)} %get-tuple-element.354, s32[]{:T(128)S(6)} %select_n.275, f32[16,4,32,512]{3,2,1,0:T(8,128)} %get-tuple-element.352, f32[16,4,32]{2,1,0:T(4,128)S(1)} %get-tuple-element.353), kind=kOutput, calls=%fused_computation.13.clone.1 | convolution fusion | flops 135528448 | bytes 8397824 | tf_op jit(solution)/shard_map/while/body/ngqk,nkgd->ngqd/dot_general | solution.py:106
  95.9 5.9 %fusion.87 = f32[16,4,32,128]{3,2,1,0:T(8,128)} fusion(f32[16,4,32,128]{3,2,1,0:T(8,128)} %get-tuple-element.338, bf16[16,512,4,128]{1,3,2,0:T(8,128)(2,1)} %get-tuple-element.354, s32[]{:T(128)S(6)} %select_n.275, f32[16,4,32,512]{3,2,1,0:T(8,128)} %get-tuple-element.352, f32[16,4,32]{2,1,0:T(4,128)S(1)} %get-tuple-element.353), kind=kOutput, calls=%fused_computation.13.clone.1 | convolution fusion | flops 135528448 | bytes 8397824 | tf_op jit(solution)/shard_map/while/body/ngqk,nkgd->ngqd/dot_general | solution.py:106
  103.3 1.3 fusion.38
  104.5 1.6 fusion.30
  106.1 0.9 copy.178
  107.0 2.1 reshape_reshape.3
  109.0 1.3 copy.140
  110.4 14.7 %all_to_all.25 = bf16[32,8,1024]{2,0,1:T(8,128)(2,1)S(1)} all-to-all(bf16[32,8,1024]{2,0,1:T(8,128)(2,1)S(1)} %copy.140), channel_id=1, replica_groups=mesh['dp'=4,'ep'=8] {'ep'}, dimensions={1} | all-to-all | bytes 1048576 | tf_op jit(solution)/shard_map/all_to_all | solution.py:209
  125.1 4.8 %fusion.71 = f32[256,2048]{1,0:T(8,128)} fusion(bf16[256,1024]{1,0:T(8,128)(2,1)S(1)} %bitcast.168, bf16[1024,2048]{1,0:T(8,128)(2,1)} %param.30), kind=kOutput, calls=%fused_computation.123 | convolution fusion | flops 1073741824 | bytes 6815744 | tf_op jit(solution)/shard_map/dot_general | solution.py:218
  131.5 39.2 %reduce-scatter.2.cloned.1.call-done = f32[32,2048]{1,0:T(8,128)} async-done(((f32[256,2048]{1,0:T(8,128)}), f32[32,2048]{1,0:T(8,128)}) %reduce-scatter.2.cloned.1.call-update) | async-done | bytes 262160 | tf_op jit(solution)/shard_map/reduce_scatter | solution.py:217
  170.7 1.2 multiply_reduce_fusion
  172.7 53.1 %all_to_all.26 = bf16[32,16,2048]{2,1,0:T(8,128)(2,1)S(1)} all-to-all(bf16[32,16,2048]{2,1,0:T(8,128)(2,1)S(1)} %bitcast.164), channel_id=1, replica_groups=mesh['dp'=4,'ep'=8] {'dp','ep'}, dimensions={0} | all-to-all | bytes 4194304 | tf_op jit(solution)/shard_map/all_to_all | solution.py:243
  225.8 5.5 %fusion.17 = f32[32,1,16,1536]{3,2,0,1:T(8,128)S(1)} fusion(bf16[32,16,2048]{2,1,0:T(8,128)(2,1)S(1)} %all_to_all.26, bf16[1,2048,1536]{2,1,0:T(8,128)(2,1)} %param.32), kind=kOutput, calls=%fused_computation.18 | convolution fusion | flops 3221225472 | bytes 11534336 | tf_op jit(solution)/shard_map/sjcd,jdf->sjcf/dot_general | solution.py:123
  231.3 3.2 %fusion.22 = bf16[32,16,2048]{2,1,0:T(8,128)(2,1)} fusion(bf16[1,768,2048]{2,1,0:T(8,128)(2,1)S(1)} %copy-done, f32[32,1,16,1536]{3,2,0,1:T(8,128)S(1)} %fusion.17), kind=kOutput, calls=%fused_computation.21 | convolution fusion | flops 1614020608 | bytes 8388608 | tf_op jit(solution)/shard_map/sjcf,jfd->sjcd/dot_general | solution.py:127
  234.5 3.8 %all-to-all-start.2 = ((bf16[32,16,2048]{2,1,0:T(8,128)(2,1)}), bf16[32,16,2048]{2,1,0:T(8,128)(2,1)}, u32[]{:S(2)}, u32[]{:S(2)}) async-start(bf16[32,16,2048]{2,1,0:T(8,128)(2,1)} %fusion.22), calls=%async_computation.3 | async-start | bytes 4194304 | tf_op jit(solution)/shard_map/all_to_all | solution.py:255
  238.4 2.0 reshape.381
  240.5 46.7 %all-to-all-done.2 = bf16[32,16,2048]{2,1,0:T(8,128)(2,1)} async-done(((bf16[32,16,2048]{2,1,0:T(8,128)(2,1)}), bf16[32,16,2048]{2,1,0:T(8,128)(2,1)}, u32[]{:S(2)}, u32[]{:S(2)}) %all-to-all-start.2) | async-done | bytes 2097184 | tf_op jit(solution)/shard_map/all_to_all | solution.py:255
  287.2 5.2 %gather_fusion = bf16[256,2048]{1,0:T(8,128)(2,1)} fusion(bf16[512,2048]{1,0:T(8,128)(2,1)} %bitcast.41, s32[1024]{0:T(1024)S(1)} %pad_clamp_fusion), kind=kCustom, calls=%fused_computation | custom fusion | bytes 2098176 | tf_op jit(solution)/shard_map/gather | solution.py:262
  292.4 2.2 fusion.25
  (108 shorter events, 21.1 us)
Async XLA Ops:
  7.2 224.2 %copy-start = (bf16[1,768,2048]{2,1,0:T(8,128)(2,1)S(1)}, bf16[1,768,2048]{2,1,0:T(8,128)(2,1)}, u32[]{:S(2)}) copy-start(bf16[1,768,2048]{2,1,0:T(8,128)(2,1)} %param.33) | copy-start | bytes 9437188
  7.2 163.5 %reduce-scatter.2.cloned.1.call-start = ((), (), s32[]{:S(2)}) async-start(), calls=%async_computation.4 | async-start | bytes 2359296 | tf_op jit(solution)/shard_map/reduce_scatter | solution.py:217
  9.9 33.7 %copy-start.16 = (pred[16,1,4]{0,2,1:T(4,128)(4,1)}, pred[16,1,4]{0,2,1:T(4,128)(4,1)S(1)}, u32[]{:S(2)}) copy-start(pred[16,1,4]{0,2,1:T(4,128)(4,1)S(1)} %get-tuple-element.177) | copy-start | bytes 196
  13.2 37.2 %copy-start.10 = (f32[16,4]{1,0:T(8,128)}, f32[16,4]{1,0:T(8,128)S(1)}, u32[]{:S(2)}) copy-start(f32[16,4]{1,0:T(8,128)S(1)} %copy.123) | copy-start | bytes 772
  14.6 13.8 %copy-start.12 = (s32[16]{0:T(128)}, s32[16]{0:T(128)S(1)}, u32[]{:S(2)}) copy-start(s32[16]{0:T(128)S(1)} %broadcast_add_fusion) | copy-start | bytes 196
  31.3 16.1 %copy-start.6 = (bf16[16,2,512]{2,1,0:T(2,128)(2,1)S(1)}, bf16[16,2,512]{2,1,0:T(2,128)(2,1)}, u32[]{:S(2)}) copy-start(bf16[16,2,512]{2,1,0:T(2,128)(2,1)} %param.22) | copy-start | bytes 98308
  31.3 16.1 %copy-start.7 = (bf16[16,2,512]{2,1,0:T(2,128)(2,1)S(1)}, bf16[16,2,512]{2,1,0:T(2,128)(2,1)}, u32[]{:S(2)}) copy-start(bf16[16,2,512]{2,1,0:T(2,128)(2,1)} %param.21) | copy-start | bytes 98308
  59.2 6.6 %copy-start.13 = (s32[16]{0:T(128)S(1)}, s32[16]{0:T(128)}, u32[]{:S(2)}) copy-start(s32[16]{0:T(128)} %copy-done.12) | copy-start | bytes 196
  75.0 3.3 %copy-start.5 = (f32[16,4,128]{2,1,0:T(4,128)S(1)}, f32[16,4,128]{2,1,0:T(4,128)}, u32[]{:S(2)}) copy-start(f32[16,4,128]{2,1,0:T(4,128)} %reshape.389) | copy-start | bytes 98308
  75.0 4.2 %copy-start.4 = (f32[16,4,128]{2,1,0:T(4,128)S(1)}, f32[16,4,128]{2,1,0:T(4,128)}, u32[]{:S(2)}) copy-start(f32[16,4,128]{2,1,0:T(4,128)} %reduce_sum.112) | copy-start | bytes 98308
  75.0 4.2 %copy-start.8 = (f32[16,1,512]{2,1,0:T(1,128)S(1)}, f32[16,1,512]{2,1,0:T(1,128)}, u32[]{:S(2)}) copy-start(f32[16,1,512]{2,1,0:T(1,128)} %get-tuple-element.185) | copy-start | bytes 98308
  75.1 4.2 %copy-start.9 = (f32[16,1,512]{2,1,0:T(1,128)S(1)}, f32[16,1,512]{2,1,0:T(1,128)}, u32[]{:S(2)}) copy-start(f32[16,1,512]{2,1,0:T(1,128)} %get-tuple-element.201) | copy-start | bytes 98308
  82.5 0.6 copy-start.2
  89.2 5.9 %copy-start.1 = (f32[16,4,32,512]{3,2,1,0:T(8,128)S(1)}, f32[16,4,32,512]{3,2,1,0:T(8,128)}, u32[]{:S(2)}) copy-start(f32[16,4,32,512]{3,2,1,0:T(8,128)} %get-tuple-element.352) | copy-start | bytes 12582916 | tf_op jit(solution)/shard_map/while
  95.8 5.9 %copy-start.1 = (f32[16,4,32,512]{3,2,1,0:T(8,128)S(1)}, f32[16,4,32,512]{3,2,1,0:T(8,128)}, u32[]{:S(2)}) copy-start(f32[16,4,32,512]{3,2,1,0:T(8,128)} %get-tuple-element.352) | copy-start | bytes 12582916 | tf_op jit(solution)/shard_map/while
  125.1 4.9 %copy-start.3 = (bf16[16,2,2048]{2,1,0:T(2,128)(2,1)S(1)}, bf16[16,2,2048]{2,1,0:T(2,128)(2,1)}, u32[]{:S(2)}) copy-start(bf16[16,2,2048]{2,1,0:T(2,128)(2,1)} %param.29) | copy-start | bytes 393220
  125.1 5.6 %copy-start.11 = (s32[16,2,8]{0,2,1:T(8,128)S(1)}, s32[16,2,8]{0,2,1:T(8,128)}, u32[]{:S(2)}) copy-start(s32[16,2,8]{0,2,1:T(8,128)} %param.34) | copy-start | bytes 3076
  129.9 42.0 %copy-start.14 = (f32[2048]{0:T(1024)S(1)}, f32[2048]{0:T(1024)}, u32[]{:S(2)}) copy-start(f32[2048]{0:T(1024)} %param.31) | copy-start | bytes 24580
  234.5 5.9 %copy-start.15 = (f32[16,2,8]{0,2,1:T(8,128)S(1)}, f32[16,2,8]{0,2,1:T(8,128)}, u32[]{:S(2)}) copy-start(f32[16,2,8]{0,2,1:T(8,128)} %param.35) | copy-start | bytes 3076
  234.5 52.7 %all-to-all-start.2 = ((bf16[32,16,2048]{2,1,0:T(8,128)(2,1)}), bf16[32,16,2048]{2,1,0:T(8,128)(2,1)}, u32[]{:S(2)}, u32[]{:S(2)}) async-start(bf16[32,16,2048]{2,1,0:T(8,128)(2,1)} %fusion.22), calls=%async_computation.3 | async-start | bytes 4194304 | tf_op jit(solution)/shard_map/all_to_all | solution.py:255
Sparse Core Ops, SparseCore 0:
  130.1 40.5 reduce-scatter.1
where the time goes:
time: 304 us; the launch traced here: 302 us
  waiting for transfers between devices  85.9 us (28%)
  local copies, waits for them, and re-layouts  67.8 us (22%)
  blocking collectives  67.8 us (22%)
  matrix products  37.7 us (12%)
  other arithmetic  24 us (8%)
  between operations  15.1 us (5%)
  starting transfers between devices  3.83 us (1%)
    all_to_all x1, blocking collectives, shards(): lax.all_to_all(outgoing.reshape(experts_all, capacity, width), ('dp', 'ep...  53.1 us
    all_to_all x1, waiting for transfers between devices, shards(): lax.all_to_all(answer.reshape(sources * experts_local, depth, width), ('d...  46.7 us
    reduce_scatter x1, waiting for transfers between devices, shards(): lax.psum_scatter(jnp.dot(spread, o_weight, preferred_element_type=jnp.flo...  39.2 us
    unnamed x37, local copies, waits for them, and re-layouts  26.2 us
    all_to_all x1, blocking collectives, shards(): lax.all_to_all(attended.reshape(rows, members, query_width // members), '...  14.7 us
    dot_general x2, matrix products, second_advance(): jnp.einsum('ngqk,nkgd->ngqd', raw.astype(jnp.bfloat16), value_block, pref...  11.8 us
    dot_general x2, matrix products, first_advance(): jnp.einsum('ngqd,nkgd->ngqk', queries, key_block, preferred_element_type=...  8.92 us
  transfers between devices with their start and end apart: 2, of which 2 were waited for; matrix products, arithmetic and copies ran while one was open for 1% of the time, Pallas kernels for 0%

commit v1 on v0

v1 whole, which is shorter than its diff:
```python
import functools
import math

import jax
import jax.numpy as jnp
from jax import lax
from jax.experimental import pallas as pl
from jax.experimental.pallas import tpu as pltpu
from jax.sharding import PartitionSpec as P

EPS = 1e-06
HEAD = 128
FIRST = 128
BLOCK = 16
TOGETHER = 4


def lanes(per_head, heads):
    return jnp.concatenate(
        [jnp.broadcast_to(per_head[:, g : g + 1], (per_head.shape[0], HEAD)) for g in range(heads)],
        axis=1,
    )


def attend_kernel(
    heads,
    group,
    lengths_ref,
    flags_ref,
    queries_ref,
    keys_new_ref,
    values_new_ref,
    importance_ref,
    flags_vector_ref,
    last_weight_ref,
    key_cache_ref,
    value_cache_ref,
    out_ref,
    keys_ref,
    values_ref,
    key_slots_ref,
    value_slots_ref,
    extra_keys_ref,
    extra_values_ref,
    slot_rows_ref,
    highest_ref,
    total_ref,
    summed_ref,
    slot_sem,
    first_sem,
    rest_sem,
):
    requests, slots, features = key_cache_ref.shape
    rest = slots - FIRST
    rows = 2 * group * heads
    scale = 1.0 / math.sqrt(HEAD)

    def slot_copies(r):
        start = pl.multiple_of(((lengths_ref[r] - 1) // BLOCK) * BLOCK, BLOCK)
        return (
            pltpu.make_async_copy(
                key_cache_ref.at[r, pl.ds(start, BLOCK)], key_slots_ref.at[r], slot_sem.at[0, r]
            ),
            pltpu.make_async_copy(
                value_cache_ref.at[r, pl.ds(start, BLOCK)], value_slots_ref.at[r], slot_sem.at[1, r]
            ),
        )

    def first_copies(r):
        return (
            pltpu.make_async_copy(
                key_cache_ref.at[r, pl.ds(0, FIRST)], keys_ref.at[r, pl.ds(0, FIRST)], first_sem.at[0, r]
            ),
            pltpu.make_async_copy(
                value_cache_ref.at[r, pl.ds(0, FIRST)],
                values_ref.at[r, pl.ds(0, FIRST)],
                first_sem.at[1, r],
            ),
        )

    def rest_copies(r):
        return (
            pltpu.make_async_copy(
                key_cache_ref.at[r, pl.ds(FIRST, rest)],
                keys_ref.at[r, pl.ds(FIRST, rest)],
                rest_sem.at[0, r],
            ),
            pltpu.make_async_copy(
                value_cache_ref.at[r, pl.ds(FIRST, rest)],
                values_ref.at[r, pl.ds(FIRST, rest)],
                rest_sem.at[1, r],
            ),
        )

    def start_slots(r, carry):
        for copy in slot_copies(r):
            copy.start()
        return carry

    def start_first(r, carry):
        for copy in first_copies(r):
            copy.start()
        return carry

    def start_rest(r, carry):
        @pl.when(lengths_ref[r] > FIRST)
        def _():
            for copy in rest_copies(r):
                copy.start()

        return carry

    lax.fori_loop(0, requests, start_slots, 0)
    lax.fori_loop(0, requests, start_first, 0)
    lax.fori_loop(0, requests, start_rest, 0)

    def take_slot(r, carry):
        for copy in slot_copies(r):
            copy.wait()
        inside = (lengths_ref[r] - 1) % BLOCK
        here = lax.broadcasted_iota(jnp.int32, (BLOCK, features), 0) == inside
        for which, block_ref in ((0, key_slots_ref), (1, value_slots_ref)):
            block = block_ref[r].astype(jnp.float32)
            slot_rows_ref[which, pl.ds(r, 1), :] = jnp.sum(
                jnp.where(here, block, 0.0), axis=0, keepdims=True
            )
        return carry

    lax.fori_loop(0, requests, take_slot, 0)

    weight = lanes(last_weight_ref[...], heads)
    importance = importance_ref[...]
    flags = flags_vector_ref[...]
    share0 = lanes(importance[:, :heads], heads)
    share1 = lanes(importance[:, heads:], heads)
    merge0 = lanes(flags[:, :heads], heads) == 1
    merge1 = lanes(flags[:, heads:], heads) == 1
    weight0 = jnp.where(merge0, weight + share0, share0)
    for which, new_ref, extra_ref in (
        (0, keys_new_ref, extra_keys_ref),
        (1, values_new_ref, extra_values_ref),
    ):
        new0 = new_ref[:, :features].astype(jnp.float32)
        new1 = new_ref[:, features:].astype(jnp.float32)
        slot = slot_rows_ref[which]
        blended0 = (weight * slot + share0 * new0) / (weight + share0)
        current = jnp.where(merge0, blended0, new0).astype(jnp.bfloat16).astype(jnp.float32)
        blended1 = (weight0 * current + share1 * new1) / (weight0 + share1)
        latest = jnp.where(merge1, blended1, new1).astype(jnp.bfloat16).astype(jnp.float32)
        extra_ref[0] = current
        extra_ref[1] = latest

    row = lax.broadcasted_iota(jnp.int32, (rows, 1), 0)
    row_head = row // (2 * group)
    second = (row // group) % 2 == 1

    def by_head(r, offset):
        result = jnp.zeros((rows, 1), jnp.int32)
        for g in range(heads):
            result = jnp.where(row_head == g, flags_ref[r * 2 * heads + offset + g], result)
        return result

    def per_head_rows(vector):
        return jnp.concatenate(
            [
                jnp.broadcast_to(vector[:, g * HEAD : (g + 1) * HEAD], (2 * group, HEAD))
                for g in range(heads)
            ],
            axis=0,
        )

    def block_scores(r, start, size, queries, limit):
        parts = []
        for g in range(heads):
            parts.append(
                lax.dot_general(
                    queries[g * 2 * group : (g + 1) * 2 * group],
                    keys_ref[r, start : start + size, g * HEAD : (g + 1) * HEAD],
                    (((1,), (1,)), ((), ())),
                    preferred_element_type=jnp.float32,
                )
            )
        scores = jnp.concatenate(parts, axis=0) * scale
        position = lax.broadcasted_iota(jnp.int32, (rows, size), 1) + start
        return jnp.where(position < limit, scores, -jnp.inf)

    def block_sums(r, start, size, raw):
        raw = raw.astype(jnp.bfloat16)
        return jnp.concatenate(
            [
                jnp.dot(
                    raw[g * 2 * group : (g + 1) * 2 * group],
                    values_ref[r, start : start + size, g * HEAD : (g + 1) * HEAD],
                    preferred_element_type=jnp.float32,
                )
                for g in range(heads)
            ],
            axis=0,
        )

    def rounded(raw):
        return raw.astype(jnp.bfloat16).astype(jnp.float32)

    def first_stage(turn, carry):
        for inner in range(TOGETHER):
            for copy in first_copies(turn * TOGETHER + inner):
                copy.wait()
        for inner in range(TOGETHER):
            r = turn * TOGETHER + inner
            queries = queries_ref[r]
            wide = queries.astype(jnp.float32)
            limit = lengths_ref[r] - by_head(r, 0)
            scores = block_scores(r, 0, FIRST, queries, limit)
            current = per_head_rows(extra_keys_ref[0, pl.ds(r, 1), :])
            latest = per_head_rows(extra_keys_ref[1, pl.ds(r, 1), :])
            current_score = jnp.sum(wide * current, axis=1, keepdims=True) * scale
            latest_score = jnp.sum(wide * latest, axis=1, keepdims=True) * scale
            hidden = second & (by_head(r, heads) == 1)
            current_score = jnp.where(hidden, -jnp.inf, current_score)
            latest_score = jnp.where(second, latest_score, -jnp.inf)
            highest = jnp.maximum(
                jnp.max(scores, axis=1, keepdims=True), jnp.maximum(current_score, latest_score)
            )
            raw = jnp.exp(scores - highest)
            current_raw = jnp.exp(current_score - highest)
            latest_raw = jnp.exp(latest_score - highest)
            total = jnp.sum(raw, axis=1, keepdims=True) + current_raw + latest_raw
            summed = (
                block_sums(r, 0, FIRST, raw)
                + rounded(current_raw) * per_head_rows(extra_values_ref[0, pl.ds(r, 1), :])
                + rounded(latest_raw) * per_head_rows(extra_values_ref[1, pl.ds(r, 1), :])
            )
            highest_ref[r] = jnp.broadcast_to(highest, (rows, HEAD))
            total_ref[r] = jnp.broadcast_to(total, (rows, HEAD))
            summed_ref[r] = summed
            out_ref[r] = (summed / total).astype(jnp.bfloat16)
        return carry

    lax.fori_loop(0, requests // TOGETHER, first_stage, 0)

    def rest_stage(r, carry):
        @pl.when(lengths_ref[r] > FIRST)
        def _():
            for copy in rest_copies(r):
                copy.wait()
            limit = lengths_ref[r] - by_head(r, 0)
            scores = block_scores(r, FIRST, rest, queries_ref[r], limit)
            former = highest_ref[r][:, :1]
            highest = jnp.maximum(jnp.max(scores, axis=1, keepdims=True), former)
            raw = jnp.exp(scores - highest)
            keep = jnp.exp(former - highest)
            total = total_ref[r][:, :1] * keep + jnp.sum(raw, axis=1, keepdims=True)
            summed = summed_ref[r] * keep + block_sums(r, FIRST, rest, raw)
            out_ref[r] = (summed / total).astype(jnp.bfloat16)

        return carry

    lax.fori_loop(0, requests, rest_stage, 0)


def attend(
    queries, keys_new, values_new, importance, merge_flags, key_cache, value_cache, last_weight, lengths
):
    requests, steps, query_width = queries.shape
    heads = last_weight.shape[1]
    features = keys_new.shape[2]
    slots = key_cache.shape[1]
    group = query_width // HEAD // heads
    rows = steps * group * heads
    grouped = (
        queries.reshape(requests, steps, heads, group, HEAD)
        .transpose(0, 2, 1, 3, 4)
        .reshape(requests, rows, HEAD)
    )
    vmem = pl.BlockSpec(memory_space=pltpu.VMEM)
    smem = pl.BlockSpec(memory_space=pltpu.SMEM)
    hbm = pl.BlockSpec(memory_space=pl.ANY)
    flags = merge_flags.reshape(requests, steps * heads)
    out = pl.pallas_call(
        functools.partial(attend_kernel, heads, group),
        out_shape=jax.ShapeDtypeStruct((requests, rows, HEAD), jnp.bfloat16),
        in_specs=[smem, smem] + [vmem] * 6 + [hbm, hbm],
        out_specs=vmem,
        scratch_shapes=[
            pltpu.VMEM((requests, slots, features), jnp.bfloat16),
            pltpu.VMEM((requests, slots, features), jnp.bfloat16),
            pltpu.VMEM((requests, BLOCK, features), jnp.bfloat16),
            pltpu.VMEM((requests, BLOCK, features), jnp.bfloat16),
            pltpu.VMEM((2, requests, features), jnp.float32),
            pltpu.VMEM((2, requests, features), jnp.float32),
            pltpu.VMEM((2, requests, features), jnp.float32),
            pltpu.VMEM((requests, rows, HEAD), jnp.float32),
            pltpu.VMEM((requests, rows, HEAD), jnp.float32),
            pltpu.VMEM((requests, rows, HEAD), jnp.float32),
            pltpu.SemaphoreType.DMA((2, requests)),
            pltpu.SemaphoreType.DMA((2, requests)),
            pltpu.SemaphoreType.DMA((2, requests)),
        ],
        compiler_params=pltpu.CompilerParams(vmem_limit_bytes=48 * 1024 * 1024),
        name="attend",
    )(
        lengths,
        flags.reshape(-1),
        grouped,
        keys_new.reshape(requests, steps * features),
        values_new.reshape(requests, steps * features),
        importance.reshape(requests, steps * heads),
        flags,
        last_weight,
        key_cache,
        value_cache,
    )
    return (
        out.reshape(requests, heads, steps, group, HEAD)
        .transpose(0, 2, 1, 3, 4)
        .reshape(requests, steps, query_width)
    )


def shards(
    queries,
    keys_new,
    values_new,
    importance,
    merge_flags,
    key_cache,
    value_cache,
    last_weight,
    lengths,
    residual,
    o_weight,
    norm_gain,
    expert_gate_up,
    expert_down,
    routes,
    route_weights,
):
    requests, steps, query_width = queries.shape
    members = lax.axis_size("ep")
    sources = lax.axis_size("dp") * members
    rows = requests * steps
    top_k = routes.shape[2]
    width = o_weight.shape[1]
    every = ("dp", "ep")
    chosen = lax.all_gather(routes.reshape(rows, top_k), every, axis=0)
    gates = lax.all_gather(route_weights.reshape(rows, top_k), every, axis=0)
    attended = attend(
        queries,
        keys_new,
        values_new,
        importance,
        merge_flags,
        key_cache,
        value_cache,
        last_weight,
        lengths,
    )
    spread = lax.all_to_all(
        attended.reshape(rows, members, query_width // members),
        "ep",
        split_axis=1,
        concat_axis=0,
        tiled=True,
    )
    spread = spread.reshape(members * rows, query_width // members)
    projected = lax.psum_scatter(
        jnp.dot(spread, o_weight, preferred_element_type=jnp.float32).astype(jnp.bfloat16),
        "ep",
        scatter_dimension=0,
        tiled=True,
    )
    mixed = residual.reshape(rows, width).astype(jnp.float32) + projected.astype(jnp.float32)
    normed = (
        mixed * lax.rsqrt(jnp.mean(mixed * mixed, axis=1, keepdims=True) + EPS) * norm_gain
    ).astype(jnp.bfloat16)
    tokens = lax.all_gather(normed, every, axis=0)
    capacity = max(2, 2 * rows * top_k // sources)
    hit = chosen == lax.axis_index(every)
    gate = jnp.sum(jnp.where(hit, gates, 0.0), axis=2)
    member = jnp.any(hit, axis=2)
    rank = jnp.cumsum(member.astype(jnp.int32), axis=1) - 1
    picking = (jnp.arange(capacity)[None, :, None] == rank[:, None, :]) & member[:, None, :]
    placing = picking.astype(jnp.bfloat16)
    arrived = jnp.einsum(
        "sct,std->scd", placing, tokens, preferred_element_type=jnp.float32
    ).astype(jnp.bfloat16)
    both = jnp.dot(
        arrived.reshape(sources * capacity, width),
        expert_gate_up[0],
        preferred_element_type=jnp.float32,
    )
    hidden_units = expert_down.shape[1]
    active = (jax.nn.silu(both[:, :hidden_units]) * both[:, hidden_units:]).astype(jnp.bfloat16)
    answer = jnp.dot(active, expert_down[0], preferred_element_type=jnp.float32)
    slot_gate = jnp.sum(jnp.where(picking, gate[:, None, :], 0.0), axis=2).reshape(-1, 1)
    answer = (answer * slot_gate).astype(jnp.bfloat16).reshape(sources, capacity, width)
    share = jnp.einsum(
        "sct,scd->std", placing, answer, preferred_element_type=jnp.float32
    ).astype(jnp.bfloat16)
    blended = lax.psum_scatter(
        share.reshape(sources * rows, width), every, scatter_dimension=0, tiled=True
    )
    layer_out = (mixed + blended.astype(jnp.float32)).astype(jnp.bfloat16)
    return (attended, layer_out.reshape(requests, steps, width))


def solution(mesh):
    return jax.shard_map(
        shards,
        mesh=mesh,
        in_specs=(
            P(("dp", "ep"), None, None),
            P(("dp", "ep"), None, None),
            P(("dp", "ep"), None, None),
            P(("dp", "ep"), None, None),
            P(("dp", "ep"), None, None),
            P(("dp", "ep"), None, None),
            P(("dp", "ep"), None, None),
            P(("dp", "ep"), None),
            P(("dp", "ep")),
            P(("dp", "ep"), None, None),
            P("ep", None),
            P(),
            P(("dp", "ep"), None, None),
            P(("dp", "ep"), None, None),
            P(("dp", "ep"), None, None),
            P(("dp", "ep"), None, None),
        ),
        out_specs=(P(("dp", "ep"), None, None), P(("dp", "ep"), None, None)),
        check_vma=False,
    )
```

time: 304 us -> 330 us (1.086)
  waiting for transfers between devices: 85.9 us -> 171 us
  local copies, waits for them, and re-layouts: 67.8 us -> 17.8 us
  blocking collectives: 67.8 us -> 93.7 us
  matrix products: 37.7 us -> 18 us
  other arithmetic: 24 us -> 4.75 us
  Pallas kernels: 0 us -> 9.19 us
  starting transfers between devices: 3.83 us -> 0.12 us
    reduce_scatter x0 -> x1, waiting for transfers between devices: none -> 136 us  [shards(): lax.psum_scatter(share.reshape(sources * rows, width), every, scatter_dim...]
    all_gather x0 -> x2, blocking collectives: none -> 78.2 us  [the longest x1 41 us: shards(): chosen = lax.all_gather(routes.reshape(rows, top_k), every, axis=0)]
    all_to_all x1 -> x0, blocking collectives: 53.1 us -> none  [shards(): lax.all_to_all(outgoing.reshape(experts_all, capacity, width), ('dp', 'ep...]
    all_to_all x1 -> x0, waiting for transfers between devices: 46.7 us -> none  [shards(): lax.all_to_all(answer.reshape(sources * experts_local, depth, width), ('d...]
    unnamed x37 -> x18, local copies, waits for them, and re-layouts: 26.2 us -> 4.6 us
    dot_general x9 -> x4, matrix products: 32.9 us -> 13.5 us  [the longest x1 5.55 us: shards(): jnp.dot(arrived.reshape(sources * capacity, width), expert_gate_up[0], pr...]
    pallas_call x0 -> x1, Pallas kernels: none -> 9.19 us  [attend(): pl.pallas_call(functools.partial(attend_kernel, heads, group), out_shape=...]
    gather x3 -> x0, local copies, waits for them, and re-layouts: 8.12 us -> none  [the longest x1 5.21 us: shards(): returned.reshape(experts_all * capacity, width)[target]]
  transfers between devices with their start and end apart: 2 -> 3, of which waited for: 2 -> 2; matrix products, arithmetic and copies ran while one was open for 1% -> 1% of each run, Pallas kernels for 0% -> 0%
where the time goes in v1:
time: 330 us; the launch traced here: 329 us
  waiting for transfers between devices  171 us (52%)
  blocking collectives  93.7 us (28%)
  matrix products  18 us (5%)
  local copies, waits for them, and re-layouts  17.8 us (5%)
  between operations  13.9 us (4%)
  Pallas kernels  9.19 us (3%)
  other arithmetic  4.75 us (1%)
    reduce_scatter x1, waiting for transfers between devices, shards(): lax.psum_scatter(share.reshape(sources * rows, width), every, scatter_dim...  136 us
    all_gather x1, blocking collectives, shards(): chosen = lax.all_gather(routes.reshape(rows, top_k), every, axis=0)  41 us
    all_gather x1, blocking collectives, shards(): gates = lax.all_gather(route_weights.reshape(rows, top_k), every, axis=0)  37.2 us
    reduce_scatter x1, waiting for transfers between devices, shards(): lax.psum_scatter(jnp.dot(spread, o_weight, preferred_element_type=jnp.flo...  34.7 us
    all_to_all x1, blocking collectives, shards(): lax.all_to_all(attended.reshape(rows, members, query_width // members), '...  15.6 us
    pallas_call x1, Pallas kernels, attend(): pl.pallas_call(functools.partial(attend_kernel, heads, group), out_shape=...  9.19 us
  transfers between devices with their start and end apart: 3, of which 2 were waited for; matrix products, arithmetic and copies ran while one was open for 1% of the time, Pallas kernels for 0%

profile of v1, /device:TPU:0, one launch (start us, length us, event | category | flops | bytes accessed | tf_op | source)
XLA Modules:
  0.0 328.7 jit_solution(17642926959527197967)
XLA Ops:
  7.2 0.0 copy-start
  7.2 0.0 reduce-scatter.3.cloned.1.call-start
  7.2 0.9 copy.35.importance_ref
  8.1 0.8 copy.37.last_weight_ref
  8.9 0.8 copy.33
  9.7 0.8 copy.36.flags_vector_ref
  10.4 0.1 reshape_reshape.6.flags_ref
  10.5 0.8 copy.44
  11.3 0.8 copy.45
  12.1 2.2 reshape.69
  14.3 1.1 copy.34
  15.4 0.0 copy-start.1
  15.4 0.6 copy-done.1
  16.0 9.2 %attend.1 = bf16[16,128,128]{2,1,0:T(8,128)(2,1)S(1)} custom-call(s32[16]{0:T(128)S(1)} %copy-done.1, s32[128]{0:T(128)S(1)} %reshape_reshape.6.flags_ref, bf16[16,128,128]{2,1,0:T(8,128)(2,1)S(1)} %bitcast.39, bf16[16,1024]{1,0:T(8,128)(2,1)S(1)} %bitcast.41, bf16[16,1024]{1,0:T(8,128)(2,1)S(1)} %bitcast.42, f32[16,8]{1,0:T(8,128)S(1)} %copy.35.importance_ref, ...), custom_call_target="tpu_custom_call" | custom-call | tf_op jit(solution)/shard_map/attend/pallas_call | solution.py:279
  25.2 0.9 copy.47
  26.1 2.1 reshape_reshape.7
  28.1 1.3 copy.39
  29.5 15.6 %all_to_all.15 = bf16[32,8,1024]{2,0,1:T(8,128)(2,1)S(1)} all-to-all(bf16[32,8,1024]{2,0,1:T(8,128)(2,1)S(1)} %copy.39), channel_id=1, replica_groups=mesh['dp'=4,'ep'=8] {'ep'}, dimensions={1} | all-to-all | bytes 1048576 | tf_op jit(solution)/shard_map/all_to_all | solution.py:358
  45.0 4.5 %convolution_convert_fusion.2 = bf16[256,2048]{1,0:T(8,128)(2,1)} fusion(bf16[256,1024]{1,0:T(8,128)(2,1)S(1)} %bitcast.49, bf16[1024,2048]{1,0:T(8,128)(2,1)} %param.26), kind=kOutput, calls=%fused_computation.6 | convolution fusion | flops 1074266112 | bytes 5767168 | tf_op jit(solution)/shard_map/dot_general | solution.py:367
  49.5 0.0 reduce-scatter.3.cloned.1.call-update
  49.6 0.0 all-gather.3.cloned.1.call-start
  49.6 0.0 copy-done.3
  49.7 34.7 %reduce-scatter.3.cloned.1.call-done = bf16[32,2048]{1,0:T(8,128)(2,1)} async-done(((bf16[256,2048]{1,0:T(8,128)(2,1)}), bf16[32,2048]{1,0:T(8,128)(2,1)}) %reduce-scatter.3.cloned.1.call-update) | async-done | bytes 131088 | tf_op jit(solution)/shard_map/reduce_scatter | solution.py:366
  84.3 1.0 multiply_reduce_fusion
  85.4 0.0 copy-done.4
  85.4 1.7 multiply_convert_fusion.1
  87.1 0.0 all-gather.3.cloned.1.call-update
  87.1 0.0 reduce-scatter.5.cloned.1.call-start
  87.1 0.1 copy.40
  87.2 0.1 copy.41
  87.3 0.8 copy.42
  88.1 0.1 copy.43
  88.1 41.0 %all_gather.12 = s32[32,32,8]{1,2,0:T(8,128)S(1)} all-gather(s32[1,32,8]{1,2,0:T(8,128)S(1)} %copy.41), channel_id=1, replica_groups=mesh['dp'=4,'ep'=8] {'dp','ep'}, dimensions={0}, use_global_device_ids=true | all-gather | bytes 33792 | tf_op jit(solution)/shard_map/all_gather | solution.py:345
  129.1 0.1 fusion.14
  129.2 0.2 reduce_window_sum.11
  129.4 37.2 %all_gather.15 = f32[32,32,8]{1,2,0:T(8,128)S(1)} all-gather(f32[1,32,8]{1,2,0:T(8,128)S(1)} %copy.43), channel_id=1, replica_groups=mesh['dp'=4,'ep'=8] {'dp','ep'}, dimensions={0}, use_global_device_ids=true | all-gather | bytes 33792 | tf_op jit(solution)/shard_map/all_gather | solution.py:346
  166.6 0.1 select_reduce_fusion.1
  166.6 0.1 select_reduce_fusion
  166.8 0.1 mul.47
  166.9 2.9 convolution_convert_fusion.1
  169.8 5.5 %fusion = f32[512,1536]{1,0:T(8,128)S(1)} fusion(bf16[512,2048]{1,0:T(8,128)(2,1)S(1)} %bitcast.48, bf16[1,2048,1536]{2,1,0:T(8,128)(2,1)} %param.28), kind=kOutput, calls=%fused_computation | convolution fusion | flops 3221225472 | bytes 11534336 | tf_op jit(solution)/shard_map/dot_general | solution.py:387
  175.3 1.9 multiply_convert_fusion
  177.2 3.2 convolution_convert_fusion
  180.4 0.0 reduce-scatter.5.cloned.1.call-update
  180.4 2.0 reshape.76
  182.4 136.5 %reduce-scatter.5.cloned.1.call-done = bf16[32,2048]{1,0:T(8,128)(2,1)} async-done(((bf16[1024,2048]{1,0:T(8,128)(2,1)}), bf16[32,2048]{1,0:T(8,128)(2,1)}) %reduce-scatter.5.cloned.1.call-update) | async-done | bytes 131088 | tf_op jit(solution)/shard_map/reduce_scatter | solution.py:400
  318.9 1.6 add_convert_fusion
  320.5 1.7 reshape.81
  (12 shorter events, 0.1 us)
Async XLA Ops:
  7.2 168.2 %copy-start = (bf16[1,768,2048]{2,1,0:T(8,128)(2,1)S(1)}, bf16[1,768,2048]{2,1,0:T(8,128)(2,1)}, u32[]{:S(2)}) copy-start(bf16[1,768,2048]{2,1,0:T(8,128)(2,1)} %param.29) | copy-start | bytes 9437188
  7.2 77.2 %reduce-scatter.3.cloned.1.call-start = ((), (), s32[]{:S(2)}) async-start(), calls=%async_computation.3 | async-start | bytes 1179648 | tf_op jit(solution)/shard_map/reduce_scatter | solution.py:366
  15.4 0.7 copy-start.1
  45.0 4.6 %copy-start.3 = (bf16[16,2,2048]{2,1,0:T(2,128)(2,1)S(1)}, bf16[16,2,2048]{2,1,0:T(2,128)(2,1)}, u32[]{:S(2)}) copy-start(bf16[16,2,2048]{2,1,0:T(2,128)(2,1)} %param.25) | copy-start | bytes 393220
  45.0 40.4 %copy-start.4 = (f32[2048]{0:T(1024)S(1)}, f32[2048]{0:T(1024)}, u32[]{:S(2)}) copy-start(f32[2048]{0:T(1024)} %param.27) | copy-start | bytes 24580
  45.0 42.1 %copy-start.5 = (s32[16,2,8]{0,2,1:T(8,128)S(1)}, s32[16,2,8]{0,2,1:T(8,128)}, u32[]{:S(2)}) copy-start(s32[16,2,8]{0,2,1:T(8,128)} %param.30) | copy-start | bytes 3076
  49.6 117.3 %all-gather.3.cloned.1.call-start = ((), (), s32[]{:S(2)}) async-start(), calls=%async_computation.5 | async-start | bytes 4325376 | tf_op jit(solution)/shard_map/all_gather | solution.py:376
  87.1 231.8 %reduce-scatter.5.cloned.1.call-start = ((), (), s32[]{:S(2)}) async-start(), calls=%async_computation.4 | async-start | bytes 4325376 | tf_op jit(solution)/shard_map/reduce_scatter | solution.py:400
  180.4 138.5 %copy-start.2 = (bf16[32,2048]{1,0:T(8,128)(2,1)S(1)}, bf16[32,2048]{1,0:T(8,128)(2,1)}, u32[]{:S(2)}) copy-start(bf16[32,2048]{1,0:T(8,128)(2,1)} %reduce-scatter.3.cloned.1.call-done) | copy-start | bytes 393220
Sparse Core Ops, SparseCore 0:
  49.7 34.6 reduce-scatter.2
  87.8 62.0 all-gather.2
  180.6 138.3 reduce-scatter.4

commit v2 on v1

--- a/solution.py
+++ b/solution.py
@@ -342,8 +342,7 @@
     top_k = routes.shape[2]
     width = o_weight.shape[1]
     every = ("dp", "ep")
-    chosen = lax.all_gather(routes.reshape(rows, top_k), every, axis=0)
-    gates = lax.all_gather(route_weights.reshape(rows, top_k), every, axis=0)
+    chosen = routes.reshape(rows, top_k)
     attended = attend(
         queries,
         keys_new,
@@ -363,20 +362,20 @@
         tiled=True,
     )
     spread = spread.reshape(members * rows, query_width // members)
-    projected = lax.psum_scatter(
-        jnp.dot(spread, o_weight, preferred_element_type=jnp.float32).astype(jnp.bfloat16),
-        "ep",
-        scatter_dimension=0,
-        tiled=True,
-    )
-    mixed = residual.reshape(rows, width).astype(jnp.float32) + projected.astype(jnp.float32)
+    terms = jnp.dot(spread, o_weight, preferred_element_type=jnp.float32).astype(jnp.bfloat16)
+    terms = lax.all_to_all(
+        terms.reshape(members, rows, width), "ep", split_axis=0, concat_axis=0, tiled=True
+    )
+    projected = jnp.sum(terms.astype(jnp.float32), axis=0)
+    mixed = residual.reshape(rows, width).astype(jnp.float32) + projected
     normed = (
         mixed * lax.rsqrt(jnp.mean(mixed * mixed, axis=1, keepdims=True) + EPS) * norm_gain
     ).astype(jnp.bfloat16)
-    tokens = lax.all_gather(normed, every, axis=0)
+    named = jnp.pad(chosen.astype(jnp.bfloat16), ((0, 0), (0, HEAD - top_k)), constant_values=-1)
+    gathered = lax.all_gather(jnp.concatenate([normed, named], axis=1), every, axis=0)
+    tokens = gathered[:, :, :width]
     capacity = max(2, 2 * rows * top_k // sources)
-    hit = chosen == lax.axis_index(every)
-    gate = jnp.sum(jnp.where(hit, gates, 0.0), axis=2)
+    hit = gathered[:, :, width : width + top_k].astype(jnp.int32) == lax.axis_index(every)
     member = jnp.any(hit, axis=2)
     rank = jnp.cumsum(member.astype(jnp.int32), axis=1) - 1
     picking = (jnp.arange(capacity)[None, :, None] == rank[:, None, :]) & member[:, None, :]
@@ -392,15 +391,21 @@
     hidden_units = expert_down.shape[1]
     active = (jax.nn.silu(both[:, :hidden_units]) * both[:, hidden_units:]).astype(jnp.bfloat16)
     answer = jnp.dot(active, expert_down[0], preferred_element_type=jnp.float32)
-    slot_gate = jnp.sum(jnp.where(picking, gate[:, None, :], 0.0), axis=2).reshape(-1, 1)
-    answer = (answer * slot_gate).astype(jnp.bfloat16).reshape(sources, capacity, width)
-    share = jnp.einsum(
-        "sct,scd->std", placing, answer, preferred_element_type=jnp.float32
-    ).astype(jnp.bfloat16)
-    blended = lax.psum_scatter(
-        share.reshape(sources * rows, width), every, scatter_dimension=0, tiled=True
-    )
-    layer_out = (mixed + blended.astype(jnp.float32)).astype(jnp.bfloat16)
+    returned = lax.all_to_all(
+        answer.astype(jnp.bfloat16).reshape(sources, capacity, width),
+        every,
+        split_axis=0,
+        concat_axis=0,
+        tiled=True,
+    )
+    sequence = jnp.arange(rows * top_k, dtype=jnp.int32)
+    flat = chosen.reshape(rows * top_k)
+    earlier = sequence[:, None] > sequence[None, :]
+    order = jnp.sum(((flat[:, None] == flat[None, :]) & earlier).astype(jnp.int32), axis=1)
+    target = flat * capacity + order
+    results = returned.reshape(sources * capacity, width)[target].reshape(rows, top_k, width)
+    blended = jnp.sum(route_weights.reshape(rows, top_k, 1) * results.astype(jnp.float32), axis=1)
+    layer_out = (mixed + blended).astype(jnp.bfloat16)
     return (attended, layer_out.reshape(requests, steps, width))
 
 

time: 330 us -> 227 us (0.69)
  blocking collectives: 93.7 us -> 16.6 us
  waiting for transfers between devices: 171 us -> 115 us
  local copies, waits for them, and re-layouts: 17.8 us -> 32.1 us
  other arithmetic: 4.75 us -> 14.7 us
  starting transfers between devices: 0.12 us -> 7.93 us
    reduce_scatter x2 -> x0, waiting for transfers between devices: 171 us -> none  [the longest x1 136 us: shards(): lax.psum_scatter(share.reshape(sources * rows, width), every, scatter_dim...]
    all_gather x2 -> x0, blocking collectives: 78.2 us -> none  [the longest x1 41 us: shards(): chosen = lax.all_gather(routes.reshape(rows, top_k), every, axis=0)]
    all_gather x1, waiting for transfers between devices: 0.01 us -> 61.4 us  [shards(): lax.all_gather(jnp.concatenate([normed, named], axis=1), every, axis=0)]
    all_to_all x0 -> x2, waiting for transfers between devices: none -> 53.7 us  [the longest x1 39.8 us: shards(): lax.all_to_all(answer.astype(jnp.bfloat16).reshape(sources, capacity, wid...]
    all_to_all x0 -> x2, starting transfers between devices: none -> 7.89 us  [the longest x1 4.23 us: shards(): lax.all_to_all(terms.reshape(members, rows, width), 'ep', split_axis=0, c...]
    reduce_sum x2 -> x3, other arithmetic: 0.19 us -> 5.93 us  [the longest x1 2.88 us: shards(): jnp.sum(route_weights.reshape(rows, top_k, 1) * results.astype(jnp.float3...]
    gather x0 -> x1, local copies, waits for them, and re-layouts: none -> 5.34 us  [shards(): returned.reshape(sources * capacity, width)[target]]
  transfers between devices with their start and end apart: 3 -> 3, of which waited for: 2 -> 3; matrix products, arithmetic and copies ran while one was open for 1% -> 5% of each run, Pallas kernels for 0% -> 0%
where the time goes in v2:
time: 227 us; the launch traced here: 225 us
  waiting for transfers between devices  115 us (51%)
  local copies, waits for them, and re-layouts  32.1 us (14%)
  blocking collectives  16.6 us (7%)
  matrix products  16.1 us (7%)
  other arithmetic  14.7 us (6%)
  between operations  14.1 us (6%)
  Pallas kernels  8.59 us (4%)
  starting transfers between devices  7.93 us (3%)
    all_gather x1, waiting for transfers between devices, shards(): lax.all_gather(jnp.concatenate([normed, named], axis=1), every, axis=0)  61.4 us
    all_to_all x1, waiting for transfers between devices, shards(): lax.all_to_all(answer.astype(jnp.bfloat16).reshape(sources, capacity, wid...  39.8 us
    all_to_all x1, blocking collectives, shards(): lax.all_to_all(attended.reshape(rows, members, query_width // members), '...  16.6 us
    all_to_all x1, waiting for transfers between devices, shards(): lax.all_to_all(terms.reshape(members, rows, width), 'ep', split_axis=0, c...  13.9 us
    pallas_call x1, Pallas kernels, attend(): pl.pallas_call(functools.partial(attend_kernel, heads, group), out_shape=...  8.59 us
    unnamed x18, local copies, waits for them, and re-layouts  6.91 us
    dot_general x1, matrix products, shards(): jnp.dot(arrived.reshape(sources * capacity, width), expert_gate_up[0], pr...  5.54 us
    gather x1, local copies, waits for them, and re-layouts, shards(): returned.reshape(sources * capacity, width)[target]  5.34 us
  transfers between devices with their start and end apart: 3, of which 3 were waited for; matrix products, arithmetic and copies ran while one was open for 5% of the time, Pallas kernels for 0%

profile of v2, /device:TPU:0, one launch (start us, length us, event | category | flops | bytes accessed | tf_op | source)
XLA Modules:
  0.0 225.3 jit_solution(10945844458666238947)
XLA Ops:
  7.2 2.4 %reshape.116 = bf16[16,2,4,16,128]{4,3,2,1,0:T(8,128)(2,1)} reshape(bf16[16,2,8192]{2,1,0:T(2,128)(2,1)} %param.16) | data formatting | bytes 1048576 | tf_op jit(solution)/shard_map/reshape | solution.py:271
  9.6 1.9 copy.47
  11.4 0.8 copy.57
  12.2 0.8 copy.58
  13.0 0.8 copy.46
  13.8 0.8 copy.48.importance_ref
  14.6 0.8 copy.49.flags_vector_ref
  15.4 0.8 copy.50.last_weight_ref
  16.1 1.0 copy-done.1
  17.2 0.7 copy-done.2
  17.8 8.6 %attend.1 = bf16[16,128,128]{2,1,0:T(8,128)(2,1)S(1)} custom-call(s32[16]{0:T(128)S(1)} %copy-done.2, s32[128]{0:T(128)S(1)} %reshape_reshape.7.flags_ref, bf16[16,128,128]{2,1,0:T(8,128)(2,1)S(1)} %bitcast.45, bf16[16,1024]{1,0:T(8,128)(2,1)S(1)} %bitcast.47, bf16[16,1024]{1,0:T(8,128)(2,1)S(1)} %bitcast.48, f32[16,8]{1,0:T(8,128)S(1)} %copy.48.importance_ref, ...), custom_call_target="tpu_custom_call" | custom-call | tf_op jit(solution)/shard_map/attend/pallas_call | solution.py:279
  26.4 0.9 copy.60
  27.3 2.1 reshape_reshape.8
  29.3 1.3 copy.52
  30.7 16.6 %all_to_all.25 = bf16[32,8,1024]{2,0,1:T(8,128)(2,1)S(1)} all-to-all(bf16[32,8,1024]{2,0,1:T(8,128)(2,1)S(1)} %copy.52), channel_id=1, replica_groups=mesh['dp'=4,'ep'=8] {'ep'}, dimensions={1} | all-to-all | bytes 1048576 | tf_op jit(solution)/shard_map/all_to_all | solution.py:357
  47.2 4.5 %convolution_convert_fusion = bf16[256,2048]{1,0:T(8,128)(2,1)} fusion(bf16[256,1024]{1,0:T(8,128)(2,1)S(1)} %bitcast.56, bf16[1024,2048]{1,0:T(8,128)(2,1)} %param.26), kind=kOutput, calls=%fused_computation.9 | convolution fusion | flops 1074266112 | bytes 5767168 | tf_op jit(solution)/shard_map/dot_general | solution.py:365
  51.8 4.2 %all-to-all-start.1 = ((bf16[8,32,2048]{2,1,0:T(8,128)(2,1)}), bf16[8,32,2048]{2,1,0:T(8,128)(2,1)}, u32[]{:S(2)}, u32[]{:S(2)}) async-start(bf16[8,32,2048]{2,1,0:T(8,128)(2,1)} %bitcast.55), calls=%async_computation.1 | async-start | bytes 2097152 | tf_op jit(solution)/shard_map/all_to_all | solution.py:366
  56.1 0.7 reshape.129
  56.8 0.6 broadcast_multiply_fusion
  57.5 13.9 %all-to-all-done.1 = bf16[8,32,2048]{2,1,0:T(8,128)(2,1)} async-done(((bf16[8,32,2048]{2,1,0:T(8,128)(2,1)}), bf16[8,32,2048]{2,1,0:T(8,128)(2,1)}, u32[]{:S(2)}, u32[]{:S(2)}) %all-to-all-start.1) | async-done | bytes 1048608 | tf_op jit(solution)/shard_map/all_to_all | solution.py:366
  71.4 2.1 convert_reduce_fusion
  73.5 1.1 reduce_sum.43
  74.9 0.6 rsqrt.12
  75.5 1.1 multiply_convert_fusion
  76.6 0.7 fusion.21
  77.3 61.4 %all-gather.3.cloned.1.call-done = bf16[1024,2176]{1,0:T(8,128)(2,1)} async-done(((bf16[32,2176]{1,0:T(8,128)(2,1)}), bf16[1024,2176]{1,0:T(8,128)(2,1)}) %all-gather.3.cloned.1.call-update) | async-done | bytes 4456464 | tf_op jit(solution)/shard_map/all_gather | solution.py:375
  138.7 1.6 fusion.16
  140.3 0.6 copy-done.4
  140.9 0.8 reduce_window_sum.11
  141.7 0.7 broadcast_add_fusion
  142.4 2.9 %fusion.9 = bf16[32,16,2048]{2,1,0:T(8,128)(2,1)S(1)} fusion(bf16[32,32,2176]{2,1,0:T(8,128)(2,1)} %bitcast.52, s32[32,32]{1,0:T(8,128)S(1)} %broadcast_add_fusion, pred[32,32]{1,0:T(8,128)(4,1)} %copy-done.4), kind=kOutput, calls=%fused_computation.8 | convolution fusion | flops 68190208 | bytes 6299648 | tf_op jit(solution)/shard_map/sct,std->scd/dot_general | solution.py:383
  145.3 5.5 %fusion = f32[512,1536]{1,0:T(8,128)S(1)} fusion(bf16[512,2048]{1,0:T(8,128)(2,1)S(1)} %bitcast.54, bf16[1,2048,1536]{2,1,0:T(8,128)(2,1)} %param.28), kind=kOutput, calls=%fused_computation.1 | convolution fusion | flops 3221225472 | bytes 11534336 | tf_op jit(solution)/shard_map/dot_general | solution.py:386
  150.9 3.1 %fusion.6 = bf16[512,2048]{1,0:T(8,128)(2,1)} fusion(bf16[1,768,2048]{2,1,0:T(8,128)(2,1)S(1)} %copy-done, f32[512,1536]{1,0:T(8,128)S(1)} %fusion), kind=kOutput, calls=%fused_computation.7 | convolution fusion | flops 1614020608 | bytes 8388608 | tf_op jit(solution)/shard_map/dot_general | solution.py:393
  154.0 3.7 %all-to-all-start.2 = ((bf16[32,16,2048]{2,1,0:T(8,128)(2,1)}), bf16[32,16,2048]{2,1,0:T(8,128)(2,1)}, u32[]{:S(2)}, u32[]{:S(2)}) async-start(bf16[32,16,2048]{2,1,0:T(8,128)(2,1)} %bitcast.53), calls=%async_computation.2 | async-start | bytes 4194304 | tf_op jit(solution)/shard_map/all_to_all | solution.py:394
  157.7 0.8 copy.56
  158.5 2.0 reshape.123
  160.4 1.4 copy.55
  161.8 1.4 mul.68
  163.2 0.7 eq.39
  163.9 0.8 copy.53
  164.6 0.9 convert_reduce_fusion.1
  165.6 0.7 compare_select_fusion
  166.2 0.6 pad_clamp_fusion
  166.8 39.8 %all-to-all-done.2 = bf16[32,16,2048]{2,1,0:T(8,128)(2,1)} async-done(((bf16[32,16,2048]{2,1,0:T(8,128)(2,1)}), bf16[32,16,2048]{2,1,0:T(8,128)(2,1)}, u32[]{:S(2)}, u32[]{:S(2)}) %all-to-all-start.2) | async-done | bytes 2097184 | tf_op jit(solution)/shard_map/all_to_all | solution.py:394
  206.6 5.3 %gather_fusion = bf16[256,2048]{1,0:T(8,128)(2,1)} fusion(bf16[512,2048]{1,0:T(8,128)(2,1)} %bitcast.17, s32[1024]{0:T(1024)} %pad_clamp_fusion), kind=kCustom, calls=%fused_computation | custom fusion | bytes 2098176 | tf_op jit(solution)/shard_map/gather | solution.py:406
  211.9 2.9 %fusion.12 = f32[32,2048]{1,0:T(8,128)} fusion(bf16[256,2048]{1,0:T(8,128)(2,1)} %gather_fusion, f32[32,8]{1,0:T(8,128)S(1)} %bitcast.57), kind=kLoop, calls=%fused_computation.11 | loop fusion | flops 1507328 | bytes 1311744 | tf_op jit(solution)/shard_map/reduce_sum | solution.py:407
  214.8 1.8 reduce_sum.48
  216.6 1.8 add_convert_fusion
  (16 shorter events, 0.5 us)
Async XLA Ops:
  7.2 143.7 %copy-start = (bf16[1,768,2048]{2,1,0:T(8,128)(2,1)S(1)}, bf16[1,768,2048]{2,1,0:T(8,128)(2,1)}, u32[]{:S(2)}) copy-start(bf16[1,768,2048]{2,1,0:T(8,128)(2,1)} %param.29) | copy-start | bytes 9437188
  16.1 1.0 copy-start.1
  17.2 0.7 copy-start.2
  47.2 8.8 %copy-start.3 = (bf16[16,2,2048]{2,1,0:T(2,128)(2,1)S(1)}, bf16[16,2,2048]{2,1,0:T(2,128)(2,1)}, u32[]{:S(2)}) copy-start(bf16[16,2,2048]{2,1,0:T(2,128)(2,1)} %param.25) | copy-start | bytes 393220
  47.2 9.6 %copy-start.5 = (s32[16,2,8]{0,2,1:T(8,128)S(1)}, s32[16,2,8]{0,2,1:T(8,128)}, u32[]{:S(2)}) copy-start(s32[16,2,8]{0,2,1:T(8,128)} %param.30) | copy-start | bytes 3076
  51.8 19.7 %all-to-all-start.1 = ((bf16[8,32,2048]{2,1,0:T(8,128)(2,1)}), bf16[8,32,2048]{2,1,0:T(8,128)(2,1)}, u32[]{:S(2)}, u32[]{:S(2)}) async-start(bf16[8,32,2048]{2,1,0:T(8,128)(2,1)} %bitcast.55), calls=%async_computation.1 | async-start | bytes 2097152 | tf_op jit(solution)/shard_map/all_to_all | solution.py:366
  56.0 82.7 %all-gather.3.cloned.1.call-start = ((), (), s32[]{:S(2)}) async-start(), calls=%async_computation.3 | async-start | bytes 4595712 | tf_op jit(solution)/shard_map/all_gather | solution.py:375
  140.3 0.6 copy-start.4
  154.0 52.6 %all-to-all-start.2 = ((bf16[32,16,2048]{2,1,0:T(8,128)(2,1)}), bf16[32,16,2048]{2,1,0:T(8,128)(2,1)}, u32[]{:S(2)}, u32[]{:S(2)}) async-start(bf16[32,16,2048]{2,1,0:T(8,128)(2,1)} %bitcast.53), calls=%async_computation.2 | async-start | bytes 4194304 | tf_op jit(solution)/shard_map/all_to_all | solution.py:394
Sparse Core Ops, SparseCore 0:
  77.4 61.2 all-gather.2

commit v3 on v2

--- a/solution.py
+++ b/solution.py
@@ -371,18 +371,24 @@
     normed = (
         mixed * lax.rsqrt(jnp.mean(mixed * mixed, axis=1, keepdims=True) + EPS) * norm_gain
     ).astype(jnp.bfloat16)
-    named = jnp.pad(chosen.astype(jnp.bfloat16), ((0, 0), (0, HEAD - top_k)), constant_values=-1)
-    gathered = lax.all_gather(jnp.concatenate([normed, named], axis=1), every, axis=0)
-    tokens = gathered[:, :, :width]
     capacity = max(2, 2 * rows * top_k // sources)
-    hit = gathered[:, :, width : width + top_k].astype(jnp.int32) == lax.axis_index(every)
-    member = jnp.any(hit, axis=2)
-    rank = jnp.cumsum(member.astype(jnp.int32), axis=1) - 1
-    picking = (jnp.arange(capacity)[None, :, None] == rank[:, None, :]) & member[:, None, :]
-    placing = picking.astype(jnp.bfloat16)
-    arrived = jnp.einsum(
-        "sct,std->scd", placing, tokens, preferred_element_type=jnp.float32
+    sequence = jnp.arange(rows * top_k, dtype=jnp.int32)
+    flat = chosen.reshape(rows * top_k)
+    earlier = sequence[:, None] > sequence[None, :]
+    order = jnp.sum(((flat[:, None] == flat[None, :]) & earlier).astype(jnp.int32), axis=1)
+    target = flat * capacity + order
+    places = jnp.arange(sources * capacity, dtype=jnp.int32)[:, None]
+    placing = jnp.any((places == target[None, :]).reshape(-1, rows, top_k), axis=2)
+    outgoing = jnp.dot(
+        placing.astype(jnp.bfloat16), normed, preferred_element_type=jnp.float32
     ).astype(jnp.bfloat16)
+    arrived = lax.all_to_all(
+        outgoing.reshape(sources, capacity, width),
+        every,
+        split_axis=0,
+        concat_axis=0,
+        tiled=True,
+    )
     both = jnp.dot(
         arrived.reshape(sources * capacity, width),
         expert_gate_up[0],
@@ -398,11 +404,6 @@
         concat_axis=0,
         tiled=True,
     )
-    sequence = jnp.arange(rows * top_k, dtype=jnp.int32)
-    flat = chosen.reshape(rows * top_k)
-    earlier = sequence[:, None] > sequence[None, :]
-    order = jnp.sum(((flat[:, None] == flat[None, :]) & earlier).astype(jnp.int32), axis=1)
-    target = flat * capacity + order
     results = returned.reshape(sources * capacity, width)[target].reshape(rows, top_k, width)
     blended = jnp.sum(route_weights.reshape(rows, top_k, 1) * results.astype(jnp.float32), axis=1)
     layer_out = (mixed + blended).astype(jnp.bfloat16)

time: 227 us -> 193 us (0.85)
  waiting for transfers between devices: 115 us -> 58.7 us
  blocking collectives: 16.6 us -> 67.9 us
  between operations: 14.1 us -> 0.83 us
  local copies, waits for them, and re-layouts: 32.1 us -> 23.2 us
  other arithmetic: 14.7 us -> 9.52 us
    all_gather x1 -> x0, waiting for transfers between devices: 61.4 us -> none  [shards(): lax.all_gather(jnp.concatenate([normed, named], axis=1), every, axis=0)]
    all_to_all x0 -> x1, blocking collectives: none -> 51.7 us  [shards(): lax.all_to_all(outgoing.reshape(sources, capacity, width), every, split_a...]
    all_to_all x1, waiting for transfers between devices: 39.8 us -> 46 us  [shards(): lax.all_to_all(answer.astype(jnp.bfloat16).reshape(sources, capacity, wid...]
    unnamed x18 -> x34, local copies, waits for them, and re-layouts: 6.91 us -> 2.03 us
    mul x2, local copies, waits for them, and re-layouts: 2.76 us -> 0.17 us  [shards(): target = flat * capacity + order]
  transfers between devices with their start and end apart: 3 -> 2, of which waited for: 3 -> 2; matrix products, arithmetic and copies ran while one was open for 5% -> 3% of each run, Pallas kernels for 0% -> 0%
where the time goes in v3:
time: 193 us; the launch traced here: 192 us
  blocking collectives  67.9 us (35%)
  waiting for transfers between devices  58.7 us (30%)
  local copies, waits for them, and re-layouts  23.2 us (12%)
  matrix products  14.9 us (8%)
  other arithmetic  9.52 us (5%)
  Pallas kernels  8.59 us (4%)
  starting transfers between devices  8.34 us (4%)
    all_to_all x1, blocking collectives, shards(): lax.all_to_all(outgoing.reshape(sources, capacity, width), every, split_a...  51.7 us
    all_to_all x1, waiting for transfers between devices, shards(): lax.all_to_all(answer.astype(jnp.bfloat16).reshape(sources, capacity, wid...  46 us
    all_to_all x1, blocking collectives, shards(): lax.all_to_all(attended.reshape(rows, members, query_width // members), '...  16.2 us
    all_to_all x1, waiting for transfers between devices, shards(): lax.all_to_all(terms.reshape(members, rows, width), 'ep', split_axis=0, c...  12.7 us
    pallas_call x1, Pallas kernels, attend(): pl.pallas_call(functools.partial(attend_kernel, heads, group), out_shape=...  8.59 us
    dot_general x1, matrix products, shards(): jnp.dot(arrived.reshape(sources * capacity, width), expert_gate_up[0], pr...  5.53 us
    gather x1, local copies, waits for them, and re-layouts, shards(): returned.reshape(sources * capacity, width)[target]  5.4 us
    dot_general x1, matrix products, shards(): jnp.dot(spread, o_weight, preferred_element_type=jnp.float32)  4.48 us
  transfers between devices with their start and end apart: 2, of which 2 were waited for; matrix products, arithmetic and copies ran while one was open for 3% of the time, Pallas kernels for 0%

profile of v3, /device:TPU:0, one launch (start us, length us, event | category | flops | bytes accessed | tf_op | source)
XLA Modules:
  0.0 191.9 jit_solution(6148068722909237104)
XLA Ops:
  0.6 0.0 copy-start
  0.7 2.4 %reshape.127 = bf16[16,2,4,16,128]{4,3,2,1,0:T(8,128)(2,1)} reshape(bf16[16,2,8192]{2,1,0:T(2,128)(2,1)} %param.16) | data formatting | bytes 1048576 | tf_op jit(solution)/shard_map/reshape | solution.py:271
  3.1 1.9 copy.47
  5.0 0.0 copy-done.7
  5.0 0.1 copy.46
  5.1 0.1 reshape_reshape.7.flags_ref
  5.2 0.1 copy.48.importance_ref
  5.3 0.1 copy.49.flags_vector_ref
  5.4 0.0 copy-done.13
  5.4 0.1 copy.50.last_weight_ref
  5.5 1.0 copy-done.1
  6.5 8.6 %attend.1 = bf16[16,128,128]{2,1,0:T(8,128)(2,1)S(1)} custom-call(s32[16]{0:T(128)S(1)} %copy-done.2, s32[128]{0:T(128)S(1)} %reshape_reshape.7.flags_ref, bf16[16,128,128]{2,1,0:T(8,128)(2,1)S(1)} %bitcast.46, bf16[16,1024]{1,0:T(8,128)(2,1)S(1)} %bitcast.48, bf16[16,1024]{1,0:T(8,128)(2,1)S(1)} %bitcast.49, f32[16,8]{1,0:T(8,128)S(1)} %copy.48.importance_ref, ...), custom_call_target="tpu_custom_call" | custom-call | tf_op jit(solution)/shard_map/attend/pallas_call | solution.py:279
  15.1 0.9 copy.60
  16.0 2.1 %reshape_reshape.8 = bf16[32,8,1024]{2,1,0:T(8,128)(2,1)} reshape(bf16[16,2,4,16,128]{4,3,2,1,0:T(8,128)(2,1)} %bitcast.51) | data formatting | bytes 1048576 | tf_op jit(solution)/shard_map/reshape;reshape | solution.py:358
  18.0 1.3 copy.52
  19.4 16.2 %all_to_all.30 = bf16[32,8,1024]{2,0,1:T(8,128)(2,1)S(1)} all-to-all(bf16[32,8,1024]{2,0,1:T(8,128)(2,1)S(1)} %copy.52), channel_id=1, replica_groups=mesh['dp'=4,'ep'=8] {'ep'}, dimensions={1} | all-to-all | bytes 1048576 | tf_op jit(solution)/shard_map/all_to_all | solution.py:357
  35.6 4.5 %convolution_convert_fusion.1 = bf16[256,2048]{1,0:T(8,128)(2,1)} fusion(bf16[256,1024]{1,0:T(8,128)(2,1)S(1)} %bitcast.56, bf16[1024,2048]{1,0:T(8,128)(2,1)} %param.26), kind=kOutput, calls=%fused_computation.7 | convolution fusion | flops 1074266112 | bytes 5767168 | tf_op jit(solution)/shard_map/dot_general | solution.py:365
  40.0 4.4 %all-to-all-start.1 = ((bf16[8,32,2048]{2,1,0:T(8,128)(2,1)}), bf16[8,32,2048]{2,1,0:T(8,128)(2,1)}, u32[]{:S(2)}, u32[]{:S(2)}) async-start(bf16[8,32,2048]{2,1,0:T(8,128)(2,1)} %bitcast.55), calls=%async_computation.1 | async-start | bytes 2097152 | tf_op jit(solution)/shard_map/all_to_all | solution.py:366
  44.4 0.1 copy.55
  44.5 0.1 eq.30
  44.6 0.2 convert_reduce_fusion.1
  44.8 0.6 copy-done.9
  45.4 0.1 reduce_sum.47
  45.5 0.1 copy.54
  45.6 0.8 reshape.141
  46.3 0.8 fusion.11
  47.2 12.7 %all-to-all-done.1 = bf16[8,32,2048]{2,1,0:T(8,128)(2,1)} async-done(((bf16[8,32,2048]{2,1,0:T(8,128)(2,1)}), bf16[8,32,2048]{2,1,0:T(8,128)(2,1)}, u32[]{:S(2)}, u32[]{:S(2)}) %all-to-all-start.1) | async-done | bytes 1048608 | tf_op jit(solution)/shard_map/all_to_all | solution.py:366
  59.8 1.4 convert_reduce_fusion
  61.2 0.9 reduce_sum.45
  62.1 1.2 multiply_reduce_fusion
  63.3 0.6 add_rsqrt_fusion
  63.9 1.3 rsqrt.12
  65.2 1.7 convolution_convert_fusion
  66.9 51.7 %all_to_all.31 = bf16[32,16,2048]{2,1,0:T(8,128)(2,1)S(1)} all-to-all(bf16[32,16,2048]{2,1,0:T(8,128)(2,1)S(1)} %bitcast.50), channel_id=1, replica_groups=mesh['dp'=4,'ep'=8] {'dp','ep'}, dimensions={0} | all-to-all | bytes 4194304 | tf_op jit(solution)/shard_map/all_to_all | solution.py:385
  118.6 5.5 %fusion = f32[512,1536]{1,0:T(8,128)S(1)} fusion(bf16[512,2048]{1,0:T(8,128)(2,1)S(1)} %bitcast.54, bf16[1,2048,1536]{2,1,0:T(8,128)(2,1)} %param.28), kind=kOutput, calls=%fused_computation.1 | convolution fusion | flops 3221225472 | bytes 11534336 | tf_op jit(solution)/shard_map/dot_general | solution.py:392
  124.1 0.0 copy-done
  124.1 3.2 %fusion.4 = bf16[512,2048]{1,0:T(8,128)(2,1)} fusion(bf16[1,768,2048]{2,1,0:T(8,128)(2,1)S(1)} %copy-done, f32[512,1536]{1,0:T(8,128)S(1)} %fusion), kind=kOutput, calls=%fused_computation.5 | convolution fusion | flops 1614020608 | bytes 8388608 | tf_op jit(solution)/shard_map/dot_general | solution.py:399
  127.3 4.0 %all-to-all-start.3 = ((bf16[32,16,2048]{2,1,0:T(8,128)(2,1)}), bf16[32,16,2048]{2,1,0:T(8,128)(2,1)}, u32[]{:S(2)}, u32[]{:S(2)}) async-start(bf16[32,16,2048]{2,1,0:T(8,128)(2,1)} %bitcast.53), calls=%async_computation.3 | async-start | bytes 4194304 | tf_op jit(solution)/shard_map/all_to_all | solution.py:400
  131.3 0.1 mul.72
  131.4 2.0 %reshape.134 = bf16[16,2,8192]{2,1,0:T(2,128)(2,1)} reshape(bf16[16,2,4,16,128]{4,3,2,1,0:T(8,128)(2,1)} %bitcast.52) | data formatting | bytes 1048576 | tf_op jit(solution)/shard_map/reshape | solution.py:316
  133.4 0.0 copy-done.11
  133.4 0.1 copy.53
  133.4 0.6 pad_clamp_fusion
  134.0 46.0 %all-to-all-done.3 = bf16[32,16,2048]{2,1,0:T(8,128)(2,1)} async-done(((bf16[32,16,2048]{2,1,0:T(8,128)(2,1)}), bf16[32,16,2048]{2,1,0:T(8,128)(2,1)}, u32[]{:S(2)}, u32[]{:S(2)}) %all-to-all-start.3) | async-done | bytes 2097184 | tf_op jit(solution)/shard_map/all_to_all | solution.py:400
  180.0 5.4 %gather_fusion = bf16[256,2048]{1,0:T(8,128)(2,1)} fusion(bf16[512,2048]{1,0:T(8,128)(2,1)} %bitcast.17, s32[1024]{0:T(1024)} %pad_clamp_fusion), kind=kCustom, calls=%fused_computation | custom fusion | bytes 2098176 | tf_op jit(solution)/shard_map/gather | solution.py:407
  185.4 2.9 %fusion.7 = f32[32,2048]{1,0:T(8,128)} fusion(bf16[256,2048]{1,0:T(8,128)(2,1)} %gather_fusion, f32[32,8]{1,0:T(8,128)S(1)} %bitcast.58), kind=kLoop, calls=%fused_computation.9 | loop fusion | flops 1507328 | bytes 1311744 | tf_op jit(solution)/shard_map/reduce_sum | solution.py:408
  188.3 1.8 reduce_sum.51
  190.1 1.8 add_convert_fusion
  (26 shorter events, 0.1 us)
Async XLA Ops:
  0.6 123.5 %copy-start = (bf16[1,768,2048]{2,1,0:T(8,128)(2,1)S(1)}, bf16[1,768,2048]{2,1,0:T(8,128)(2,1)}, u32[]{:S(2)}) copy-start(bf16[1,768,2048]{2,1,0:T(8,128)(2,1)} %param.29) | copy-start | bytes 9437188
  0.6 4.3 %copy-start.6 = (bf16[16,2,512]{2,1,0:T(2,128)(2,1)S(1)}, bf16[16,2,512]{2,1,0:T(2,128)(2,1)}, u32[]{:S(2)}) copy-start(bf16[16,2,512]{2,1,0:T(2,128)(2,1)} %param.17) | copy-start | bytes 98308
  0.7 4.3 %copy-start.7 = (bf16[16,2,512]{2,1,0:T(2,128)(2,1)S(1)}, bf16[16,2,512]{2,1,0:T(2,128)(2,1)}, u32[]{:S(2)}) copy-start(bf16[16,2,512]{2,1,0:T(2,128)(2,1)} %param.18) | copy-start | bytes 98308
  0.7 4.3 %copy-start.8 = (s32[16,2,4]{0,2,1:T(4,128)S(1)}, s32[16,2,4]{0,2,1:T(4,128)}, u32[]{:S(2)}) copy-start(s32[16,2,4]{0,2,1:T(4,128)} %param.20) | copy-start | bytes 1540
  0.7 4.5 %copy-start.12 = (f32[16,2,4]{0,2,1:T(4,128)S(1)}, f32[16,2,4]{0,2,1:T(4,128)}, u32[]{:S(2)}) copy-start(f32[16,2,4]{0,2,1:T(4,128)} %param.19) | copy-start | bytes 1540
  0.7 4.7 %copy-start.13 = (f32[16,4]{0,1:T(4,128)S(1)}, f32[16,4]{0,1:T(4,128)}, u32[]{:S(2)}) copy-start(f32[16,4]{0,1:T(4,128)} %param.23) | copy-start | bytes 772
  0.7 4.8 %copy-start.2 = (s32[16]{0:T(128)S(1)}, s32[16]{0:T(128)}, u32[]{:S(2)}) copy-start(s32[16]{0:T(128)} %lengths_ref.1) | copy-start | bytes 196
  5.5 1.0 copy-start.1
  40.0 4.4 %copy-start.5 = (s32[16,2,8]{0,2,1:T(8,128)S(1)}, s32[16,2,8]{0,2,1:T(8,128)}, u32[]{:S(2)}) copy-start(s32[16,2,8]{0,2,1:T(8,128)} %param.30) | copy-start | bytes 3076
  40.0 5.5 %copy-start.4 = (bf16[16,2,2048]{2,1,0:T(2,128)(2,1)S(1)}, bf16[16,2,2048]{2,1,0:T(2,128)(2,1)}, u32[]{:S(2)}) copy-start(bf16[16,2,2048]{2,1,0:T(2,128)(2,1)} %param.25) | copy-start | bytes 393220
  40.0 19.8 %all-to-all-start.1 = ((bf16[8,32,2048]{2,1,0:T(8,128)(2,1)}), bf16[8,32,2048]{2,1,0:T(8,128)(2,1)}, u32[]{:S(2)}, u32[]{:S(2)}) async-start(bf16[8,32,2048]{2,1,0:T(8,128)(2,1)} %bitcast.55), calls=%async_computation.1 | async-start | bytes 2097152 | tf_op jit(solution)/shard_map/all_to_all | solution.py:366
  44.8 0.6 copy-start.9
  127.3 6.0 %copy-start.11 = (f32[16,2,8]{0,2,1:T(8,128)S(1)}, f32[16,2,8]{0,2,1:T(8,128)}, u32[]{:S(2)}) copy-start(f32[16,2,8]{0,2,1:T(8,128)} %param.31) | copy-start | bytes 3076
  127.3 6.1 %copy-start.10 = (s32[256]{0:T(256)S(1)}, s32[256]{0:T(256)}, u32[]{:S(2)}) copy-start(s32[256]{0:T(256)} %copy-done.9) | copy-start | bytes 3076
  127.3 52.7 %all-to-all-start.3 = ((bf16[32,16,2048]{2,1,0:T(8,128)(2,1)}), bf16[32,16,2048]{2,1,0:T(8,128)(2,1)}, u32[]{:S(2)}, u32[]{:S(2)}) async-start(bf16[32,16,2048]{2,1,0:T(8,128)(2,1)} %bitcast.53), calls=%async_computation.3 | async-start | bytes 4194304 | tf_op jit(solution)/shard_map/all_to_all | solution.py:400
  180.0 10.1 %copy-start.3 = (f32[16,2,2048]{2,1,0:T(2,128)S(1)}, f32[16,2,2048]{2,1,0:T(2,128)}, u32[]{:S(2)}) copy-start(f32[16,2,2048]{2,1,0:T(2,128)} %reduce_sum.45) | copy-start | bytes 786436

commit v4 on v3

--- a/solution.py
+++ b/solution.py
@@ -404,8 +404,14 @@
         concat_axis=0,
         tiled=True,
     )
-    results = returned.reshape(sources * capacity, width)[target].reshape(rows, top_k, width)
-    blended = jnp.sum(route_weights.reshape(rows, top_k, 1) * results.astype(jnp.float32), axis=1)
+    at_place = places[:, 0] == target.reshape(rows, top_k, 1)
+    gate = jnp.sum(jnp.where(at_place, route_weights.reshape(rows, top_k, 1), 0.0), axis=1)
+    coarse = lax.reduce_precision(gate, 8, 7)
+    halves = jnp.concatenate([coarse, gate - coarse], axis=0).astype(jnp.bfloat16)
+    terms = jnp.dot(
+        halves, returned.reshape(sources * capacity, width), preferred_element_type=jnp.float32
+    )
+    blended = terms[:rows] + terms[rows:]
     layer_out = (mixed + blended).astype(jnp.bfloat16)
     return (attended, layer_out.reshape(requests, steps, width))
 

time: 193 us -> 184 us (0.953)
  local copies, waits for them, and re-layouts: 23.2 us -> 14.9 us
  other arithmetic: 9.52 us -> 5.61 us
  matrix products: 14.9 us -> 17 us
    gather x1 -> x0, local copies, waits for them, and re-layouts: 5.4 us -> none  [shards(): returned.reshape(sources * capacity, width)[target]]
    reduce_sum x1, other arithmetic: 2.88 us -> 0.22 us  [shards(): jnp.sum(jnp.where(at_place, route_weights.reshape(rows, top_k, 1), 0.0),...]
    dot_general x0 -> x1, matrix products: none -> 2.07 us  [shards(): jnp.dot(halves, returned.reshape(sources * capacity, width), preferred_el...]
  transfers between devices with their start and end apart: 2 -> 2, of which waited for: 2 -> 2; matrix products, arithmetic and copies ran while one was open for 3% -> 2% of each run, Pallas kernels for 0% -> 0%
where the time goes in v4:
time: 184 us; the launch traced here: 182 us
  blocking collectives  66.7 us (36%)
  waiting for transfers between devices  59.8 us (32%)
  matrix products  17 us (9%)
  local copies, waits for them, and re-layouts  14.9 us (8%)
  Pallas kernels  9.19 us (5%)
  starting transfers between devices  8.17 us (4%)
  other arithmetic  5.61 us (3%)
    all_to_all x1, blocking collectives, shards(): lax.all_to_all(outgoing.reshape(sources, capacity, width), every, split_a...  51.3 us
    all_to_all x1, waiting for transfers between devices, shards(): lax.all_to_all(answer.astype(jnp.bfloat16).reshape(sources, capacity, wid...  46.5 us
    all_to_all x1, blocking collectives, shards(): lax.all_to_all(attended.reshape(rows, members, query_width // members), '...  15.4 us
    all_to_all x1, waiting for transfers between devices, shards(): lax.all_to_all(terms.reshape(members, rows, width), 'ep', split_axis=0, c...  13.3 us
    pallas_call x1, Pallas kernels, attend(): pl.pallas_call(functools.partial(attend_kernel, heads, group), out_shape=...  9.19 us
    dot_general x1, matrix products, shards(): jnp.dot(arrived.reshape(sources * capacity, width), expert_gate_up[0], pr...  5.53 us
    dot_general x1, matrix products, shards(): jnp.dot(spread, o_weight, preferred_element_type=jnp.float32)  4.48 us
    all_to_all x1, starting transfers between devices, shards(): lax.all_to_all(terms.reshape(members, rows, width), 'ep', split_axis=0, c...  4.37 us
  transfers between devices with their start and end apart: 2, of which 2 were waited for; matrix products, arithmetic and copies ran while one was open for 2% of the time, Pallas kernels for 0%

profile of v4, /device:TPU:0, one launch (start us, length us, event | category | flops | bytes accessed | tf_op | source)
XLA Modules:
  0.0 182.1 jit_solution(7412055306463351372)
XLA Ops:
  0.6 0.0 copy-start
  0.6 0.0 copy-start.6
  0.7 0.0 copy-start.7
  0.7 0.0 copy-start.8
  0.7 0.0 copy-start.10
  0.7 0.0 copy-start.11
  0.7 0.0 copy-start.2
  0.7 2.4 %reshape.107 = bf16[16,2,4,16,128]{4,3,2,1,0:T(8,128)(2,1)} reshape(bf16[16,2,8192]{2,1,0:T(2,128)(2,1)} %param.16) | data formatting | bytes 1048576 | tf_op jit(solution)/shard_map/reshape | solution.py:271
  3.1 1.9 %copy.45 = bf16[16,2,4,16,128]{4,3,1,2,0:T(8,128)(2,1)} copy(bf16[16,2,4,16,128]{4,3,2,1,0:T(8,128)(2,1)} %reshape.107) | data formatting | bytes 1048576 | tf_op jit(solution)/shard_map/reshape | solution.py:271
  5.0 0.0 copy-done.6
  5.0 0.1 copy.44
  5.1 0.1 reshape_reshape.7.flags_ref
  5.2 0.1 copy.46.importance_ref
  5.3 0.1 copy.47.flags_vector_ref
  5.4 0.1 copy.48.last_weight_ref
  5.5 1.0 copy-done.1
  6.5 9.2 %attend.1 = bf16[16,128,128]{2,1,0:T(8,128)(2,1)S(1)} custom-call(s32[16]{0:T(128)S(1)} %copy-done.2, s32[128]{0:T(128)S(1)} %reshape_reshape.7.flags_ref, bf16[16,128,128]{2,1,0:T(8,128)(2,1)S(1)} %bitcast.42, bf16[16,1024]{1,0:T(8,128)(2,1)S(1)} %bitcast.44, bf16[16,1024]{1,0:T(8,128)(2,1)S(1)} %bitcast.45, f32[16,8]{1,0:T(8,128)S(1)} %copy.46.importance_ref, ...), custom_call_target="tpu_custom_call" | custom-call | tf_op jit(solution)/shard_map/attend/pallas_call | solution.py:279
  15.7 0.9 copy.57
  16.6 2.1 %reshape_reshape.8 = bf16[32,8,1024]{2,1,0:T(8,128)(2,1)} reshape(bf16[16,2,4,16,128]{4,3,2,1,0:T(8,128)(2,1)} %bitcast.47) | data formatting | bytes 1048576 | tf_op jit(solution)/shard_map/reshape;reshape | solution.py:358
  18.6 1.3 copy.50
  19.9 15.4 %all_to_all.30 = bf16[32,8,1024]{2,0,1:T(8,128)(2,1)S(1)} all-to-all(bf16[32,8,1024]{2,0,1:T(8,128)(2,1)S(1)} %copy.50), channel_id=1, replica_groups=mesh['dp'=4,'ep'=8] {'ep'}, dimensions={1} | all-to-all | bytes 1048576 | tf_op jit(solution)/shard_map/all_to_all | solution.py:357
  35.3 4.5 %convolution_convert_fusion.1 = bf16[256,2048]{1,0:T(8,128)(2,1)} fusion(bf16[256,1024]{1,0:T(8,128)(2,1)S(1)} %bitcast.52, bf16[1024,2048]{1,0:T(8,128)(2,1)} %param.26), kind=kOutput, calls=%fused_computation.6 | convolution fusion | flops 1074266112 | bytes 5767168 | tf_op jit(solution)/shard_map/dot_general | solution.py:365
  39.8 4.4 %all-to-all-start.1 = ((bf16[8,32,2048]{2,1,0:T(8,128)(2,1)}), bf16[8,32,2048]{2,1,0:T(8,128)(2,1)}, u32[]{:S(2)}, u32[]{:S(2)}) async-start(bf16[8,32,2048]{2,1,0:T(8,128)(2,1)} %bitcast.51), calls=%async_computation.1 | async-start | bytes 2097152 | tf_op jit(solution)/shard_map/all_to_all | solution.py:366
  44.2 0.7 reshape.122
  44.9 0.1 copy.52
  45.0 0.1 eq.43
  45.1 0.2 convert_reduce_fusion.1
  45.3 0.1 reduce_sum.42
  45.4 0.1 copy.51
  45.5 0.9 fusion.10
  46.3 13.3 %all-to-all-done.1 = bf16[8,32,2048]{2,1,0:T(8,128)(2,1)} async-done(((bf16[8,32,2048]{2,1,0:T(8,128)(2,1)}), bf16[8,32,2048]{2,1,0:T(8,128)(2,1)}, u32[]{:S(2)}, u32[]{:S(2)}) %all-to-all-start.1) | async-done | bytes 1048608 | tf_op jit(solution)/shard_map/all_to_all | solution.py:366
  59.6 1.4 convert_reduce_fusion
  61.0 0.8 reduce_sum.44
  61.8 1.7 add.39
  63.5 1.2 multiply_reduce_fusion
  64.7 0.1 rsqrt.12
  64.8 1.7 convolution_convert_fusion
  66.5 51.3 %all_to_all.31 = bf16[32,16,2048]{2,1,0:T(8,128)(2,1)S(1)} all-to-all(bf16[32,16,2048]{2,1,0:T(8,128)(2,1)S(1)} %bitcast.46), channel_id=1, replica_groups=mesh['dp'=4,'ep'=8] {'dp','ep'}, dimensions={0} | all-to-all | bytes 4194304 | tf_op jit(solution)/shard_map/all_to_all | solution.py:385
  117.8 5.5 %fusion = f32[512,1536]{1,0:T(8,128)S(1)} fusion(bf16[512,2048]{1,0:T(8,128)(2,1)S(1)} %bitcast.50, bf16[1,2048,1536]{2,1,0:T(8,128)(2,1)} %param.28), kind=kOutput, calls=%fused_computation | convolution fusion | flops 3221225472 | bytes 11534336 | tf_op jit(solution)/shard_map/dot_general | solution.py:392
  123.4 3.2 %fusion.4 = bf16[512,2048]{1,0:T(8,128)(2,1)} fusion(bf16[1,768,2048]{2,1,0:T(8,128)(2,1)S(1)} %copy-done, f32[512,1536]{1,0:T(8,128)S(1)} %fusion), kind=kOutput, calls=%fused_computation.4 | convolution fusion | flops 1614020608 | bytes 8388608 | tf_op jit(solution)/shard_map/dot_general | solution.py:399
  126.6 3.8 %all-to-all-start.3 = ((bf16[32,16,2048]{2,1,0:T(8,128)(2,1)}), bf16[32,16,2048]{2,1,0:T(8,128)(2,1)}, u32[]{:S(2)}, u32[]{:S(2)}) async-start(bf16[32,16,2048]{2,1,0:T(8,128)(2,1)} %bitcast.49), calls=%async_computation.3 | async-start | bytes 4194304 | tf_op jit(solution)/shard_map/all_to_all | solution.py:400
  130.4 2.0 %reshape.114 = bf16[16,2,8192]{2,1,0:T(2,128)(2,1)} reshape(bf16[16,2,4,16,128]{4,3,2,1,0:T(8,128)(2,1)} %bitcast.48) | data formatting | bytes 1048576 | tf_op jit(solution)/shard_map/reshape | solution.py:316
  132.4 0.0 copy-done.9
  132.4 0.1 copy.53
  132.4 0.2 select_reduce_fusion
  132.7 46.5 %all-to-all-done.3 = bf16[32,16,2048]{2,1,0:T(8,128)(2,1)} async-done(((bf16[32,16,2048]{2,1,0:T(8,128)(2,1)}), bf16[32,16,2048]{2,1,0:T(8,128)(2,1)}, u32[]{:S(2)}, u32[]{:S(2)}) %all-to-all-start.3) | async-done | bytes 2097184 | tf_op jit(solution)/shard_map/all_to_all | solution.py:400
  179.2 2.1 %fusion.17 = f32[64,2048]{1,0:T(8,128)S(1)} fusion(bf16[512,2048]{1,0:T(8,128)(2,1)} %bitcast.17, bf16[32,512]{1,0:T(8,128)(2,1)S(1)} %get-tuple-element.3, bf16[32,512]{1,0:T(8,128)(2,1)S(1)} %get-tuple-element.2), kind=kOutput, calls=%fused_computation.29 | convolution fusion | flops 134348800 | bytes 2686976 | tf_op jit(solution)/shard_map/dot_general | solution.py:411
  181.4 0.8 reshape.121
  (21 shorter events, 0.1 us)
Async XLA Ops:
  0.6 122.7 %copy-start = (bf16[1,768,2048]{2,1,0:T(8,128)(2,1)S(1)}, bf16[1,768,2048]{2,1,0:T(8,128)(2,1)}, u32[]{:S(2)}) copy-start(bf16[1,768,2048]{2,1,0:T(8,128)(2,1)} %param.29) | copy-start | bytes 9437188
  0.6 4.3 %copy-start.6 = (bf16[16,2,512]{2,1,0:T(2,128)(2,1)S(1)}, bf16[16,2,512]{2,1,0:T(2,128)(2,1)}, u32[]{:S(2)}) copy-start(bf16[16,2,512]{2,1,0:T(2,128)(2,1)} %param.17) | copy-start | bytes 98308
  0.7 4.3 %copy-start.7 = (bf16[16,2,512]{2,1,0:T(2,128)(2,1)S(1)}, bf16[16,2,512]{2,1,0:T(2,128)(2,1)}, u32[]{:S(2)}) copy-start(bf16[16,2,512]{2,1,0:T(2,128)(2,1)} %param.18) | copy-start | bytes 98308
  0.7 4.3 %copy-start.8 = (s32[16,2,4]{0,2,1:T(4,128)S(1)}, s32[16,2,4]{0,2,1:T(4,128)}, u32[]{:S(2)}) copy-start(s32[16,2,4]{0,2,1:T(4,128)} %param.20) | copy-start | bytes 1540
  0.7 4.5 %copy-start.10 = (f32[16,2,4]{0,2,1:T(4,128)S(1)}, f32[16,2,4]{0,2,1:T(4,128)}, u32[]{:S(2)}) copy-start(f32[16,2,4]{0,2,1:T(4,128)} %param.19) | copy-start | bytes 1540
  0.7 4.7 %copy-start.11 = (f32[16,4]{0,1:T(4,128)S(1)}, f32[16,4]{0,1:T(4,128)}, u32[]{:S(2)}) copy-start(f32[16,4]{0,1:T(4,128)} %param.23) | copy-start | bytes 772
  0.7 4.8 %copy-start.2 = (s32[16]{0:T(128)S(1)}, s32[16]{0:T(128)}, u32[]{:S(2)}) copy-start(s32[16]{0:T(128)} %lengths_ref.1) | copy-start | bytes 196
  5.5 1.0 copy-start.1
  39.8 4.4 %copy-start.4 = (bf16[16,2,2048]{2,1,0:T(2,128)(2,1)S(1)}, bf16[16,2,2048]{2,1,0:T(2,128)(2,1)}, u32[]{:S(2)}) copy-start(bf16[16,2,2048]{2,1,0:T(2,128)(2,1)} %param.25) | copy-start | bytes 393220
  39.8 5.1 %copy-start.5 = (s32[16,2,8]{0,2,1:T(8,128)S(1)}, s32[16,2,8]{0,2,1:T(8,128)}, u32[]{:S(2)}) copy-start(s32[16,2,8]{0,2,1:T(8,128)} %param.30) | copy-start | bytes 3076
  39.8 19.8 %all-to-all-start.1 = ((bf16[8,32,2048]{2,1,0:T(8,128)(2,1)}), bf16[8,32,2048]{2,1,0:T(8,128)(2,1)}, u32[]{:S(2)}, u32[]{:S(2)}) async-start(bf16[8,32,2048]{2,1,0:T(8,128)(2,1)} %bitcast.51), calls=%async_computation.1 | async-start | bytes 2097152 | tf_op jit(solution)/shard_map/all_to_all | solution.py:366
  126.6 5.8 %copy-start.9 = (f32[16,2,8]{0,2,1:T(8,128)S(1)}, f32[16,2,8]{0,2,1:T(8,128)}, u32[]{:S(2)}) copy-start(f32[16,2,8]{0,2,1:T(8,128)} %param.31) | copy-start | bytes 3076
  126.6 52.7 %all-to-all-start.3 = ((bf16[32,16,2048]{2,1,0:T(8,128)(2,1)}), bf16[32,16,2048]{2,1,0:T(8,128)(2,1)}, u32[]{:S(2)}, u32[]{:S(2)}) async-start(bf16[32,16,2048]{2,1,0:T(8,128)(2,1)} %bitcast.49), calls=%async_computation.3 | async-start | bytes 4194304 | tf_op jit(solution)/shard_map/all_to_all | solution.py:400
  130.4 50.9 %copy-start.3 = (f32[32,2048]{1,0:T(8,128)S(1)}, f32[32,2048]{1,0:T(8,128)}, u32[]{:S(2)}) copy-start(f32[32,2048]{1,0:T(8,128)} %add.39) | copy-start | bytes 786436
